TPU v7x, 128 devices: a whole 4x4x4 slice. The times are simulated.
128 devices in a mesh: ctx: 32 (over x, y, core), segment: 2 (over z_hi), mp: 2 (over z_lo).
Axes of the slice: x: 4, y: 4, z: 4 (z_hi: 2, z_lo: 2; z = z_hi * 2 + z_lo), core: 2. Of those that a mesh axis runs over, the one named last changes fastest.
Arguments:
- head_inputs: bfloat16 [32768, 4096], P('ctx', ('segment', 'mp')), may hold values from -0.25 to 0.25
- gate_input: bfloat16 [32768, 4096], P('ctx', ('segment', 'mp')), may hold values from -6 to 6
- state_write: bfloat16 [32768, 512], P('ctx', ('segment', 'mp')), may hold values from -6 to 6
- state_read: bfloat16 [32768, 512], P('ctx', ('segment', 'mp')), may hold values from -6 to 6
- log_decay: float32 [32768, 64], P('ctx', ('segment', 'mp')), may hold values from -1.5 to 0
- norm_gain: float32 [4096], P(('segment', 'mp')), may hold values from 0.1 to 1.9
- out_weight: bfloat16 [4096, 4096], P(('segment', 'mp'), 'ctx'), may hold values from -0.09375 to 0.09375
- residual: bfloat16 [32768, 4096], P(('ctx', 'segment', 'mp')), may hold values from -6 to 6
Outputs:
- layer_out: bfloat16 [32768, 4096], P(('ctx', 'segment', 'mp'))
All inputs are finite; a program needn't handle non-finite values.
Results may differ from a plain program's by a relative error of at most 0.014.
Values may be sent and summed in bfloat16 or wider, within the bound.
A program may use at most 128 MiB of HBM per device.

v0:
```python
import jax
import jax.numpy as jnp
from jax import lax
from jax.sharding import PartitionSpec as P

HEAD_DIM = 64
STATE = 128
SPAN = 256


def from_behind(block, axis, distance):
    devices = range(lax.axis_size(axis))
    route = [(i - distance, i) for i in devices if i - distance in devices]
    return lax.ppermute(block, axis, route)


def per_device(
    head_inputs, gate_input, state_write, state_read, log_decay, norm_gain, out_weight, residual
):
    rows_here = head_inputs.shape[0]
    heads_here = log_decay.shape[1]
    spans = rows_here // SPAN
    features = heads_here * HEAD_DIM
    head_rows = head_inputs.reshape(spans, SPAN, heads_here, HEAD_DIM)
    write_rows = state_write.reshape(spans, SPAN, STATE)
    read_rows = state_read.reshape(spans, SPAN, STATE)
    cumulative = jnp.cumsum(log_decay.reshape(spans, SPAN, heads_here), axis=1)
    cum_heads = jnp.swapaxes(cumulative, 1, 2)
    rows_index = lax.broadcasted_iota(jnp.int32, (SPAN, SPAN), 0)
    cols_index = lax.broadcasted_iota(jnp.int32, (SPAN, SPAN), 1)
    lower_mask = rows_index >= cols_index
    differences = cum_heads[:, :, :, None] - cum_heads[:, :, None, :]
    decay_matrix = jnp.exp(jnp.where(lower_mask[None, None], differences, -jnp.inf))
    scores = jnp.einsum("cin,cjn->cij", read_rows, write_rows, preferred_element_type=jnp.float32)
    mixing = (decay_matrix * scores[:, None]).astype(jnp.bfloat16)
    within_block = jnp.einsum(
        "chij,cjhp->cihp", mixing, head_rows, preferred_element_type=jnp.float32
    )
    final_log = cumulative[:, -1, :]
    weights = jnp.exp(final_log[:, None, :] - cumulative)
    weighted = (head_rows * weights[..., None]).astype(jnp.bfloat16).reshape(spans, SPAN, features)
    fresh_state = jnp.einsum(
        "cjn,cjk->cnk", write_rows, weighted, preferred_element_type=jnp.float32
    )
    span_decay = jnp.repeat(jnp.exp(final_log), HEAD_DIM, axis=1)

    def local_step(carried, pieces):
        state_now, through = carried
        fresh_piece, decay_piece = pieces
        advanced = (decay_piece[None, :] * state_now + fresh_piece, through * decay_piece)
        return (advanced, (state_now, through))

    start_carry = (jnp.zeros((STATE, features), jnp.float32), jnp.ones((features,), jnp.float32))
    (local_final, local_decay), (entering, enter_decay) = lax.scan(
        local_step, start_carry, (fresh_state, span_decay)
    )
    relay_turns = lax.axis_size("ctx") - 1

    def relay(turn_index, arriving):
        leaving = local_decay[None, :] * arriving + local_final
        return from_behind(leaving, "ctx", 1)

    incoming = lax.fori_loop(0, relay_turns, relay, jnp.zeros_like(local_final))
    block_states = entering + enter_decay[:, None, :] * incoming[None]
    readout = jnp.einsum(
        "cin,cnk->cik",
        read_rows,
        block_states.astype(jnp.bfloat16),
        preferred_element_type=jnp.float32,
    )
    carried_part = (
        readout.reshape(spans, SPAN, heads_here, HEAD_DIM) * jnp.exp(cumulative)[..., None]
    )
    mixed_heads = (within_block + carried_part).reshape(rows_here, features)
    gated = mixed_heads * jax.nn.silu(gate_input.astype(jnp.float32))
    factor = lax.rsqrt(jnp.mean(gated * gated, axis=1, keepdims=True) + 1e-05)
    normed = (gated * factor * norm_gain[None, :]).astype(jnp.bfloat16)
    projected = jnp.dot(
        normed,
        lax.all_gather(out_weight, "ctx", axis=1, tiled=True),
        preferred_element_type=jnp.float32,
    )
    summed = lax.psum_scatter(
        projected.astype(jnp.bfloat16), ("segment", "mp"), scatter_dimension=0, tiled=True
    ).astype(jnp.float32)
    return (residual.astype(jnp.float32) + summed).astype(jnp.bfloat16)


def solution(mesh):
    placed = (
        P("ctx", ("segment", "mp")),
        P("ctx", ("segment", "mp")),
        P("ctx", ("segment", "mp")),
        P("ctx", ("segment", "mp")),
        P("ctx", ("segment", "mp")),
        P(("segment", "mp")),
        P(("segment", "mp"), "ctx"),
        P(("ctx", "segment", "mp"), None),
    )
    return jax.shard_map(
        per_device,
        mesh=mesh,
        in_specs=placed,
        out_specs=P(("ctx", "segment", "mp"), None),
        check_vma=False,
    )
```

profile of v0, /device:TPU:1, one launch (start us, length us, event | category | flops | bytes accessed | tf_op | source)
XLA Modules:
  0.0 567.6 jit_solution(3960878688965413938)
XLA Ops:
  10.7 6.4 %reshape.89 = bf16[4,256,16,64]{3,2,1,0:T(8,128)(2,1)} reshape(bf16[1024,1024]{1,0:T(8,128)(2,1)} %param.12) | data formatting | bytes 4194304 | tf_op jit(solution)/shard_map/reshape | solution.py:24
  25.7 9.8 %while.28 = (s32[]{:T(128)}, f32[128,1024]{1,0:T(8,128)S(1)}, f32[1024]{0:T(1024)S(1)}, f32[4,128,1024]{2,1,0:T(8,128)}, f32[4,1024]{1,0:T(4,128)S(1)}, /*index=...) while((s32[]{:T(128)}, f32[128,1024]{1,0:T(8,128)S(1)}, ...), condition=%wide.region_3.4_spmd.clone, body=%wide.region_2.3_spmd.clone.sunk | while | flops 526339 | bytes 4756085 | solution.py:54
  35.6 362.8 %while.27 = (s32[]{:T(128)}, f32[128,1024]{1,0:T(8,128)S(1)}, f32[1024]{0:T(1024)S(1)}, f32[128,1024]{1,0:T(8,128)S(1)}, s32[]{:T(128)}) while((s32[]{:T(128)}, f32[128,1024]{1,0:T(8,128)S(1)}, f32[1024]{0:T(1024)S(1)}, f32[128,1024]{1,0:T(8,128)S(1)}, s32[]{:T(128)}) %tuple.46), condition=%wide.region_5.6_spmd, body=%wide.region_4.5_spmd.sunk | while | flops 262146 | bytes 3674213 | solution.py:63
  40.3 9.5 %collective-permute-done = f32[128,1024]{1,0:T(8,128)S(1)} collective-permute-done((f32[128,1024]{1,0:T(8,128)S(1)}, f32[128,1024]{1,0:T(8,128)S(1)}, u32[]{:S(2)}, u32[]{:S(2)}) %collective-permute-start) | collective-permute-done | bytes 524320 | tf_op jit(solution)/shard_map/while/body/eval_jaxpr/ppermute | solution.py:14
  54.2 15.2 %collective-permute-done = f32[128,1024]{1,0:T(8,128)S(1)} collective-permute-done((f32[128,1024]{1,0:T(8,128)S(1)}, f32[128,1024]{1,0:T(8,128)S(1)}, u32[]{:S(2)}, u32[]{:S(2)}) %collective-permute-start) | collective-permute-done | bytes 524320 | tf_op jit(solution)/shard_map/while/body/eval_jaxpr/ppermute | solution.py:14
  73.9 6.1 %collective-permute-done = f32[128,1024]{1,0:T(8,128)S(1)} collective-permute-done((f32[128,1024]{1,0:T(8,128)S(1)}, f32[128,1024]{1,0:T(8,128)S(1)}, u32[]{:S(2)}, u32[]{:S(2)}) %collective-permute-start) | collective-permute-done | bytes 524320 | tf_op jit(solution)/shard_map/while/body/eval_jaxpr/ppermute | solution.py:14
  84.5 6.1 %collective-permute-done = f32[128,1024]{1,0:T(8,128)S(1)} collective-permute-done((f32[128,1024]{1,0:T(8,128)S(1)}, f32[128,1024]{1,0:T(8,128)S(1)}, u32[]{:S(2)}, u32[]{:S(2)}) %collective-permute-start) | collective-permute-done | bytes 524320 | tf_op jit(solution)/shard_map/while/body/eval_jaxpr/ppermute | solution.py:14
  95.1 6.1 %collective-permute-done = f32[128,1024]{1,0:T(8,128)S(1)} collective-permute-done((f32[128,1024]{1,0:T(8,128)S(1)}, f32[128,1024]{1,0:T(8,128)S(1)}, u32[]{:S(2)}, u32[]{:S(2)}) %collective-permute-start) | collective-permute-done | bytes 524320 | tf_op jit(solution)/shard_map/while/body/eval_jaxpr/ppermute | solution.py:14
  105.6 6.1 %collective-permute-done = f32[128,1024]{1,0:T(8,128)S(1)} collective-permute-done((f32[128,1024]{1,0:T(8,128)S(1)}, f32[128,1024]{1,0:T(8,128)S(1)}, u32[]{:S(2)}, u32[]{:S(2)}) %collective-permute-start) | collective-permute-done | bytes 524320 | tf_op jit(solution)/shard_map/while/body/eval_jaxpr/ppermute | solution.py:14
  116.2 6.1 %collective-permute-done = f32[128,1024]{1,0:T(8,128)S(1)} collective-permute-done((f32[128,1024]{1,0:T(8,128)S(1)}, f32[128,1024]{1,0:T(8,128)S(1)}, u32[]{:S(2)}, u32[]{:S(2)}) %collective-permute-start) | collective-permute-done | bytes 524320 | tf_op jit(solution)/shard_map/while/body/eval_jaxpr/ppermute | solution.py:14
  126.8 6.1 %collective-permute-done = f32[128,1024]{1,0:T(8,128)S(1)} collective-permute-done((f32[128,1024]{1,0:T(8,128)S(1)}, f32[128,1024]{1,0:T(8,128)S(1)}, u32[]{:S(2)}, u32[]{:S(2)}) %collective-permute-start) | collective-permute-done | bytes 524320 | tf_op jit(solution)/shard_map/while/body/eval_jaxpr/ppermute | solution.py:14
  137.4 6.1 %collective-permute-done = f32[128,1024]{1,0:T(8,128)S(1)} collective-permute-done((f32[128,1024]{1,0:T(8,128)S(1)}, f32[128,1024]{1,0:T(8,128)S(1)}, u32[]{:S(2)}, u32[]{:S(2)}) %collective-permute-start) | collective-permute-done | bytes 524320 | tf_op jit(solution)/shard_map/while/body/eval_jaxpr/ppermute | solution.py:14
  147.9 6.1 %collective-permute-done = f32[128,1024]{1,0:T(8,128)S(1)} collective-permute-done((f32[128,1024]{1,0:T(8,128)S(1)}, f32[128,1024]{1,0:T(8,128)S(1)}, u32[]{:S(2)}, u32[]{:S(2)}) %collective-permute-start) | collective-permute-done | bytes 524320 | tf_op jit(solution)/shard_map/while/body/eval_jaxpr/ppermute | solution.py:14
  158.5 6.1 %collective-permute-done = f32[128,1024]{1,0:T(8,128)S(1)} collective-permute-done((f32[128,1024]{1,0:T(8,128)S(1)}, f32[128,1024]{1,0:T(8,128)S(1)}, u32[]{:S(2)}, u32[]{:S(2)}) %collective-permute-start) | collective-permute-done | bytes 524320 | tf_op jit(solution)/shard_map/while/body/eval_jaxpr/ppermute | solution.py:14
  169.1 6.1 %collective-permute-done = f32[128,1024]{1,0:T(8,128)S(1)} collective-permute-done((f32[128,1024]{1,0:T(8,128)S(1)}, f32[128,1024]{1,0:T(8,128)S(1)}, u32[]{:S(2)}, u32[]{:S(2)}) %collective-permute-start) | collective-permute-done | bytes 524320 | tf_op jit(solution)/shard_map/while/body/eval_jaxpr/ppermute | solution.py:14
  179.7 6.1 %collective-permute-done = f32[128,1024]{1,0:T(8,128)S(1)} collective-permute-done((f32[128,1024]{1,0:T(8,128)S(1)}, f32[128,1024]{1,0:T(8,128)S(1)}, u32[]{:S(2)}, u32[]{:S(2)}) %collective-permute-start) | collective-permute-done | bytes 524320 | tf_op jit(solution)/shard_map/while/body/eval_jaxpr/ppermute | solution.py:14
  190.2 6.1 %collective-permute-done = f32[128,1024]{1,0:T(8,128)S(1)} collective-permute-done((f32[128,1024]{1,0:T(8,128)S(1)}, f32[128,1024]{1,0:T(8,128)S(1)}, u32[]{:S(2)}, u32[]{:S(2)}) %collective-permute-start) | collective-permute-done | bytes 524320 | tf_op jit(solution)/shard_map/while/body/eval_jaxpr/ppermute | solution.py:14
  200.8 6.1 %collective-permute-done = f32[128,1024]{1,0:T(8,128)S(1)} collective-permute-done((f32[128,1024]{1,0:T(8,128)S(1)}, f32[128,1024]{1,0:T(8,128)S(1)}, u32[]{:S(2)}, u32[]{:S(2)}) %collective-permute-start) | collective-permute-done | bytes 524320 | tf_op jit(solution)/shard_map/while/body/eval_jaxpr/ppermute | solution.py:14
  211.4 6.1 %collective-permute-done = f32[128,1024]{1,0:T(8,128)S(1)} collective-permute-done((f32[128,1024]{1,0:T(8,128)S(1)}, f32[128,1024]{1,0:T(8,128)S(1)}, u32[]{:S(2)}, u32[]{:S(2)}) %collective-permute-start) | collective-permute-done | bytes 524320 | tf_op jit(solution)/shard_map/while/body/eval_jaxpr/ppermute | solution.py:14
  221.9 6.1 %collective-permute-done = f32[128,1024]{1,0:T(8,128)S(1)} collective-permute-done((f32[128,1024]{1,0:T(8,128)S(1)}, f32[128,1024]{1,0:T(8,128)S(1)}, u32[]{:S(2)}, u32[]{:S(2)}) %collective-permute-start) | collective-permute-done | bytes 524320 | tf_op jit(solution)/shard_map/while/body/eval_jaxpr/ppermute | solution.py:14
  271.6 6.5 %collective-permute-start = (f32[128,1024]{1,0:T(8,128)S(1)}, f32[128,1024]{1,0:T(8,128)S(1)}, u32[]{:S(2)}, u32[]{:S(2)}) collective-permute-start(f32[128,1024]{1,0:T(8,128)S(1)} %multiply_add_fusion.2), channel_id=1, source_target_pairs={{0,4},{4,8},{8,12},{12,16},{16,20},{20,24},{24,28},{28,32},{32,36}... | collective-permute-start | bytes 1572872 | tf_op jit(solution)/shard_map/while/body/eval_jaxpr/ppermute | solution.py:14
  284.3 6.5 %collective-permute-start = (f32[128,1024]{1,0:T(8,128)S(1)}, f32[128,1024]{1,0:T(8,128)S(1)}, u32[]{:S(2)}, u32[]{:S(2)}) collective-permute-start(f32[128,1024]{1,0:T(8,128)S(1)} %multiply_add_fusion.2), channel_id=1, source_target_pairs={{0,4},{4,8},{8,12},{12,16},{16,20},{20,24},{24,28},{28,32},{32,36}... | collective-permute-start | bytes 1572872 | tf_op jit(solution)/shard_map/while/body/eval_jaxpr/ppermute | solution.py:14
  296.9 6.5 %collective-permute-start = (f32[128,1024]{1,0:T(8,128)S(1)}, f32[128,1024]{1,0:T(8,128)S(1)}, u32[]{:S(2)}, u32[]{:S(2)}) collective-permute-start(f32[128,1024]{1,0:T(8,128)S(1)} %multiply_add_fusion.2), channel_id=1, source_target_pairs={{0,4},{4,8},{8,12},{12,16},{16,20},{20,24},{24,28},{28,32},{32,36}... | collective-permute-start | bytes 1572872 | tf_op jit(solution)/shard_map/while/body/eval_jaxpr/ppermute | solution.py:14
  309.6 6.5 %collective-permute-start = (f32[128,1024]{1,0:T(8,128)S(1)}, f32[128,1024]{1,0:T(8,128)S(1)}, u32[]{:S(2)}, u32[]{:S(2)}) collective-permute-start(f32[128,1024]{1,0:T(8,128)S(1)} %multiply_add_fusion.2), channel_id=1, source_target_pairs={{0,4},{4,8},{8,12},{12,16},{16,20},{20,24},{24,28},{28,32},{32,36}... | collective-permute-start | bytes 1572872 | tf_op jit(solution)/shard_map/while/body/eval_jaxpr/ppermute | solution.py:14
  322.3 6.5 %collective-permute-start = (f32[128,1024]{1,0:T(8,128)S(1)}, f32[128,1024]{1,0:T(8,128)S(1)}, u32[]{:S(2)}, u32[]{:S(2)}) collective-permute-start(f32[128,1024]{1,0:T(8,128)S(1)} %multiply_add_fusion.2), channel_id=1, source_target_pairs={{0,4},{4,8},{8,12},{12,16},{16,20},{20,24},{24,28},{28,32},{32,36}... | collective-permute-start | bytes 1572872 | tf_op jit(solution)/shard_map/while/body/eval_jaxpr/ppermute | solution.py:14
  335.0 6.5 %collective-permute-start = (f32[128,1024]{1,0:T(8,128)S(1)}, f32[128,1024]{1,0:T(8,128)S(1)}, u32[]{:S(2)}, u32[]{:S(2)}) collective-permute-start(f32[128,1024]{1,0:T(8,128)S(1)} %multiply_add_fusion.2), channel_id=1, source_target_pairs={{0,4},{4,8},{8,12},{12,16},{16,20},{20,24},{24,28},{28,32},{32,36}... | collective-permute-start | bytes 1572872 | tf_op jit(solution)/shard_map/while/body/eval_jaxpr/ppermute | solution.py:14
  347.7 6.5 %collective-permute-start = (f32[128,1024]{1,0:T(8,128)S(1)}, f32[128,1024]{1,0:T(8,128)S(1)}, u32[]{:S(2)}, u32[]{:S(2)}) collective-permute-start(f32[128,1024]{1,0:T(8,128)S(1)} %multiply_add_fusion.2), channel_id=1, source_target_pairs={{0,4},{4,8},{8,12},{12,16},{16,20},{20,24},{24,28},{28,32},{32,36}... | collective-permute-start | bytes 1572872 | tf_op jit(solution)/shard_map/while/body/eval_jaxpr/ppermute | solution.py:14
  360.4 6.5 %collective-permute-start = (f32[128,1024]{1,0:T(8,128)S(1)}, f32[128,1024]{1,0:T(8,128)S(1)}, u32[]{:S(2)}, u32[]{:S(2)}) collective-permute-start(f32[128,1024]{1,0:T(8,128)S(1)} %multiply_add_fusion.2), channel_id=1, source_target_pairs={{0,4},{4,8},{8,12},{12,16},{16,20},{20,24},{24,28},{28,32},{32,36}... | collective-permute-start | bytes 1572872 | tf_op jit(solution)/shard_map/while/body/eval_jaxpr/ppermute | solution.py:14
  373.0 6.5 %collective-permute-start = (f32[128,1024]{1,0:T(8,128)S(1)}, f32[128,1024]{1,0:T(8,128)S(1)}, u32[]{:S(2)}, u32[]{:S(2)}) collective-permute-start(f32[128,1024]{1,0:T(8,128)S(1)} %multiply_add_fusion.2), channel_id=1, source_target_pairs={{0,4},{4,8},{8,12},{12,16},{16,20},{20,24},{24,28},{28,32},{32,36}... | collective-permute-start | bytes 1572872 | tf_op jit(solution)/shard_map/while/body/eval_jaxpr/ppermute | solution.py:14
  385.7 6.5 %collective-permute-start = (f32[128,1024]{1,0:T(8,128)S(1)}, f32[128,1024]{1,0:T(8,128)S(1)}, u32[]{:S(2)}, u32[]{:S(2)}) collective-permute-start(f32[128,1024]{1,0:T(8,128)S(1)} %multiply_add_fusion.2), channel_id=1, source_target_pairs={{0,4},{4,8},{8,12},{12,16},{16,20},{20,24},{24,28},{28,32},{32,36}... | collective-permute-start | bytes 1572872 | tf_op jit(solution)/shard_map/while/body/eval_jaxpr/ppermute | solution.py:14
  418.8 15.9 %convolution_convert_fusion = bf16[1024,4096]{1,0:T(8,128)(2,1)} fusion(bf16[1024,4096]{1,0:T(8,128)(2,1)} %all-gather.2.cloned.1.call-done, f32[1024]{0:T(1024)S(1)} %copy-done.5, f32[1024]{0:T(1024)S(1)} %add_rsqrt_fusion, f32[1024,1024]{0,1:T(8,128)} %bitcast.72, bf16[1024,1024]{0,1:T(8,128)(2,1)S(1)} %copy.42), kind=kOutput, calls=%fused_computation.13 | convolution fusion | flops 8603566080 | bytes 23076864 | tf_op jit(solution)/shard_map/dot_general | solution.py:78
  434.7 122.3 %reduce-scatter.2.cloned.1.call-done = bf16[256,4096]{1,0:T(8,128)(2,1)} async-done(((bf16[1024,4096]{1,0:T(8,128)(2,1)}), bf16[256,4096]{1,0:T(8,128)(2,1)}) %reduce-scatter.2.cloned.1.call-update) | async-done | bytes 2097168 | tf_op jit(solution)/shard_map/reduce_scatter | solution.py:83
  (142 shorter events, 227.4 us)
Async XLA Ops:
  6.5 412.2 %all-gather.2.cloned.1.call-start = ((), (), s32[]{:S(2)}) async-start(), calls=%async_computation.1 | async-start | bytes 8650752 | tf_op jit(solution)/shard_map/all_gather | solution.py:80
  7.3 549.8 %reduce-scatter.2.cloned.1.call-start = ((), (), s32[]{:S(2)}) async-start(), calls=%async_computation.2 | async-start | bytes 10485760 | tf_op jit(solution)/shard_map/reduce_scatter | solution.py:83
  35.6 14.1 %collective-permute-start = (f32[128,1024]{1,0:T(8,128)S(1)}, f32[128,1024]{1,0:T(8,128)S(1)}, u32[]{:S(2)}, u32[]{:S(2)}) collective-permute-start(f32[128,1024]{1,0:T(8,128)S(1)} %multiply_add_fusion.2), channel_id=1, source_target_pairs={{0,4},{4,8},{8,12},{12,16},{16,20},{20,24},{24,28},{28,32},{32,36}... | collective-permute-start | bytes 1572872 | tf_op jit(solution)/shard_map/while/body/eval_jaxpr/ppermute | solution.py:14
  49.8 19.6 %collective-permute-start = (f32[128,1024]{1,0:T(8,128)S(1)}, f32[128,1024]{1,0:T(8,128)S(1)}, u32[]{:S(2)}, u32[]{:S(2)}) collective-permute-start(f32[128,1024]{1,0:T(8,128)S(1)} %multiply_add_fusion.2), channel_id=1, source_target_pairs={{0,4},{4,8},{8,12},{12,16},{16,20},{20,24},{24,28},{28,32},{32,36}... | collective-permute-start | bytes 1572872 | tf_op jit(solution)/shard_map/while/body/eval_jaxpr/ppermute | solution.py:14
  69.5 10.5 %collective-permute-start = (f32[128,1024]{1,0:T(8,128)S(1)}, f32[128,1024]{1,0:T(8,128)S(1)}, u32[]{:S(2)}, u32[]{:S(2)}) collective-permute-start(f32[128,1024]{1,0:T(8,128)S(1)} %multiply_add_fusion.2), channel_id=1, source_target_pairs={{0,4},{4,8},{8,12},{12,16},{16,20},{20,24},{24,28},{28,32},{32,36}... | collective-permute-start | bytes 1572872 | tf_op jit(solution)/shard_map/while/body/eval_jaxpr/ppermute | solution.py:14
  80.1 10.5 %collective-permute-start = (f32[128,1024]{1,0:T(8,128)S(1)}, f32[128,1024]{1,0:T(8,128)S(1)}, u32[]{:S(2)}, u32[]{:S(2)}) collective-permute-start(f32[128,1024]{1,0:T(8,128)S(1)} %multiply_add_fusion.2), channel_id=1, source_target_pairs={{0,4},{4,8},{8,12},{12,16},{16,20},{20,24},{24,28},{28,32},{32,36}... | collective-permute-start | bytes 1572872 | tf_op jit(solution)/shard_map/while/body/eval_jaxpr/ppermute | solution.py:14
  90.7 10.5 %collective-permute-start = (f32[128,1024]{1,0:T(8,128)S(1)}, f32[128,1024]{1,0:T(8,128)S(1)}, u32[]{:S(2)}, u32[]{:S(2)}) collective-permute-start(f32[128,1024]{1,0:T(8,128)S(1)} %multiply_add_fusion.2), channel_id=1, source_target_pairs={{0,4},{4,8},{8,12},{12,16},{16,20},{20,24},{24,28},{28,32},{32,36}... | collective-permute-start | bytes 1572872 | tf_op jit(solution)/shard_map/while/body/eval_jaxpr/ppermute | solution.py:14
  101.2 10.5 %collective-permute-start = (f32[128,1024]{1,0:T(8,128)S(1)}, f32[128,1024]{1,0:T(8,128)S(1)}, u32[]{:S(2)}, u32[]{:S(2)}) collective-permute-start(f32[128,1024]{1,0:T(8,128)S(1)} %multiply_add_fusion.2), channel_id=1, source_target_pairs={{0,4},{4,8},{8,12},{12,16},{16,20},{20,24},{24,28},{28,32},{32,36}... | collective-permute-start | bytes 1572872 | tf_op jit(solution)/shard_map/while/body/eval_jaxpr/ppermute | solution.py:14
  111.8 10.5 %collective-permute-start = (f32[128,1024]{1,0:T(8,128)S(1)}, f32[128,1024]{1,0:T(8,128)S(1)}, u32[]{:S(2)}, u32[]{:S(2)}) collective-permute-start(f32[128,1024]{1,0:T(8,128)S(1)} %multiply_add_fusion.2), channel_id=1, source_target_pairs={{0,4},{4,8},{8,12},{12,16},{16,20},{20,24},{24,28},{28,32},{32,36}... | collective-permute-start | bytes 1572872 | tf_op jit(solution)/shard_map/while/body/eval_jaxpr/ppermute | solution.py:14
  122.4 10.5 %collective-permute-start = (f32[128,1024]{1,0:T(8,128)S(1)}, f32[128,1024]{1,0:T(8,128)S(1)}, u32[]{:S(2)}, u32[]{:S(2)}) collective-permute-start(f32[128,1024]{1,0:T(8,128)S(1)} %multiply_add_fusion.2), channel_id=1, source_target_pairs={{0,4},{4,8},{8,12},{12,16},{16,20},{20,24},{24,28},{28,32},{32,36}... | collective-permute-start | bytes 1572872 | tf_op jit(solution)/shard_map/while/body/eval_jaxpr/ppermute | solution.py:14
  133.0 10.5 %collective-permute-start = (f32[128,1024]{1,0:T(8,128)S(1)}, f32[128,1024]{1,0:T(8,128)S(1)}, u32[]{:S(2)}, u32[]{:S(2)}) collective-permute-start(f32[128,1024]{1,0:T(8,128)S(1)} %multiply_add_fusion.2), channel_id=1, source_target_pairs={{0,4},{4,8},{8,12},{12,16},{16,20},{20,24},{24,28},{28,32},{32,36}... | collective-permute-start | bytes 1572872 | tf_op jit(solution)/shard_map/while/body/eval_jaxpr/ppermute | solution.py:14
  143.5 10.5 %collective-permute-start = (f32[128,1024]{1,0:T(8,128)S(1)}, f32[128,1024]{1,0:T(8,128)S(1)}, u32[]{:S(2)}, u32[]{:S(2)}) collective-permute-start(f32[128,1024]{1,0:T(8,128)S(1)} %multiply_add_fusion.2), channel_id=1, source_target_pairs={{0,4},{4,8},{8,12},{12,16},{16,20},{20,24},{24,28},{28,32},{32,36}... | collective-permute-start | bytes 1572872 | tf_op jit(solution)/shard_map/while/body/eval_jaxpr/ppermute | solution.py:14
  154.1 10.5 %collective-permute-start = (f32[128,1024]{1,0:T(8,128)S(1)}, f32[128,1024]{1,0:T(8,128)S(1)}, u32[]{:S(2)}, u32[]{:S(2)}) collective-permute-start(f32[128,1024]{1,0:T(8,128)S(1)} %multiply_add_fusion.2), channel_id=1, source_target_pairs={{0,4},{4,8},{8,12},{12,16},{16,20},{20,24},{24,28},{28,32},{32,36}... | collective-permute-start | bytes 1572872 | tf_op jit(solution)/shard_map/while/body/eval_jaxpr/ppermute | solution.py:14
  164.7 10.5 %collective-permute-start = (f32[128,1024]{1,0:T(8,128)S(1)}, f32[128,1024]{1,0:T(8,128)S(1)}, u32[]{:S(2)}, u32[]{:S(2)}) collective-permute-start(f32[128,1024]{1,0:T(8,128)S(1)} %multiply_add_fusion.2), channel_id=1, source_target_pairs={{0,4},{4,8},{8,12},{12,16},{16,20},{20,24},{24,28},{28,32},{32,36}... | collective-permute-start | bytes 1572872 | tf_op jit(solution)/shard_map/while/body/eval_jaxpr/ppermute | solution.py:14
  175.3 10.5 %collective-permute-start = (f32[128,1024]{1,0:T(8,128)S(1)}, f32[128,1024]{1,0:T(8,128)S(1)}, u32[]{:S(2)}, u32[]{:S(2)}) collective-permute-start(f32[128,1024]{1,0:T(8,128)S(1)} %multiply_add_fusion.2), channel_id=1, source_target_pairs={{0,4},{4,8},{8,12},{12,16},{16,20},{20,24},{24,28},{28,32},{32,36}... | collective-permute-start | bytes 1572872 | tf_op jit(solution)/shard_map/while/body/eval_jaxpr/ppermute | solution.py:14
  185.8 10.5 %collective-permute-start = (f32[128,1024]{1,0:T(8,128)S(1)}, f32[128,1024]{1,0:T(8,128)S(1)}, u32[]{:S(2)}, u32[]{:S(2)}) collective-permute-start(f32[128,1024]{1,0:T(8,128)S(1)} %multiply_add_fusion.2), channel_id=1, source_target_pairs={{0,4},{4,8},{8,12},{12,16},{16,20},{20,24},{24,28},{28,32},{32,36}... | collective-permute-start | bytes 1572872 | tf_op jit(solution)/shard_map/while/body/eval_jaxpr/ppermute | solution.py:14
  196.4 10.5 %collective-permute-start = (f32[128,1024]{1,0:T(8,128)S(1)}, f32[128,1024]{1,0:T(8,128)S(1)}, u32[]{:S(2)}, u32[]{:S(2)}) collective-permute-start(f32[128,1024]{1,0:T(8,128)S(1)} %multiply_add_fusion.2), channel_id=1, source_target_pairs={{0,4},{4,8},{8,12},{12,16},{16,20},{20,24},{24,28},{28,32},{32,36}... | collective-permute-start | bytes 1572872 | tf_op jit(solution)/shard_map/while/body/eval_jaxpr/ppermute | solution.py:14
  207.0 10.5 %collective-permute-start = (f32[128,1024]{1,0:T(8,128)S(1)}, f32[128,1024]{1,0:T(8,128)S(1)}, u32[]{:S(2)}, u32[]{:S(2)}) collective-permute-start(f32[128,1024]{1,0:T(8,128)S(1)} %multiply_add_fusion.2), channel_id=1, source_target_pairs={{0,4},{4,8},{8,12},{12,16},{16,20},{20,24},{24,28},{28,32},{32,36}... | collective-permute-start | bytes 1572872 | tf_op jit(solution)/shard_map/while/body/eval_jaxpr/ppermute | solution.py:14
  217.5 10.5 %collective-permute-start = (f32[128,1024]{1,0:T(8,128)S(1)}, f32[128,1024]{1,0:T(8,128)S(1)}, u32[]{:S(2)}, u32[]{:S(2)}) collective-permute-start(f32[128,1024]{1,0:T(8,128)S(1)} %multiply_add_fusion.2), channel_id=1, source_target_pairs={{0,4},{4,8},{8,12},{12,16},{16,20},{20,24},{24,28},{28,32},{32,36}... | collective-permute-start | bytes 1572872 | tf_op jit(solution)/shard_map/while/body/eval_jaxpr/ppermute | solution.py:14
  228.1 10.5 %collective-permute-start = (f32[128,1024]{1,0:T(8,128)S(1)}, f32[128,1024]{1,0:T(8,128)S(1)}, u32[]{:S(2)}, u32[]{:S(2)}) collective-permute-start(f32[128,1024]{1,0:T(8,128)S(1)} %multiply_add_fusion.2), channel_id=1, source_target_pairs={{0,4},{4,8},{8,12},{12,16},{16,20},{20,24},{24,28},{28,32},{32,36}... | collective-permute-start | bytes 1572872 | tf_op jit(solution)/shard_map/while/body/eval_jaxpr/ppermute | solution.py:14
  249.3 10.5 %collective-permute-start = (f32[128,1024]{1,0:T(8,128)S(1)}, f32[128,1024]{1,0:T(8,128)S(1)}, u32[]{:S(2)}, u32[]{:S(2)}) collective-permute-start(f32[128,1024]{1,0:T(8,128)S(1)} %multiply_add_fusion.2), channel_id=1, source_target_pairs={{0,4},{4,8},{8,12},{12,16},{16,20},{20,24},{24,28},{28,32},{32,36}... | collective-permute-start | bytes 1572872 | tf_op jit(solution)/shard_map/while/body/eval_jaxpr/ppermute | solution.py:14
  259.8 11.7 %collective-permute-start = (f32[128,1024]{1,0:T(8,128)S(1)}, f32[128,1024]{1,0:T(8,128)S(1)}, u32[]{:S(2)}, u32[]{:S(2)}) collective-permute-start(f32[128,1024]{1,0:T(8,128)S(1)} %multiply_add_fusion.2), channel_id=1, source_target_pairs={{0,4},{4,8},{8,12},{12,16},{16,20},{20,24},{24,28},{28,32},{32,36}... | collective-permute-start | bytes 1572872 | tf_op jit(solution)/shard_map/while/body/eval_jaxpr/ppermute | solution.py:14
  271.6 12.6 %collective-permute-start = (f32[128,1024]{1,0:T(8,128)S(1)}, f32[128,1024]{1,0:T(8,128)S(1)}, u32[]{:S(2)}, u32[]{:S(2)}) collective-permute-start(f32[128,1024]{1,0:T(8,128)S(1)} %multiply_add_fusion.2), channel_id=1, source_target_pairs={{0,4},{4,8},{8,12},{12,16},{16,20},{20,24},{24,28},{28,32},{32,36}... | collective-permute-start | bytes 1572872 | tf_op jit(solution)/shard_map/while/body/eval_jaxpr/ppermute | solution.py:14
  284.3 12.6 %collective-permute-start = (f32[128,1024]{1,0:T(8,128)S(1)}, f32[128,1024]{1,0:T(8,128)S(1)}, u32[]{:S(2)}, u32[]{:S(2)}) collective-permute-start(f32[128,1024]{1,0:T(8,128)S(1)} %multiply_add_fusion.2), channel_id=1, source_target_pairs={{0,4},{4,8},{8,12},{12,16},{16,20},{20,24},{24,28},{28,32},{32,36}... | collective-permute-start | bytes 1572872 | tf_op jit(solution)/shard_map/while/body/eval_jaxpr/ppermute | solution.py:14
  296.9 12.6 %collective-permute-start = (f32[128,1024]{1,0:T(8,128)S(1)}, f32[128,1024]{1,0:T(8,128)S(1)}, u32[]{:S(2)}, u32[]{:S(2)}) collective-permute-start(f32[128,1024]{1,0:T(8,128)S(1)} %multiply_add_fusion.2), channel_id=1, source_target_pairs={{0,4},{4,8},{8,12},{12,16},{16,20},{20,24},{24,28},{28,32},{32,36}... | collective-permute-start | bytes 1572872 | tf_op jit(solution)/shard_map/while/body/eval_jaxpr/ppermute | solution.py:14
  309.6 12.6 %collective-permute-start = (f32[128,1024]{1,0:T(8,128)S(1)}, f32[128,1024]{1,0:T(8,128)S(1)}, u32[]{:S(2)}, u32[]{:S(2)}) collective-permute-start(f32[128,1024]{1,0:T(8,128)S(1)} %multiply_add_fusion.2), channel_id=1, source_target_pairs={{0,4},{4,8},{8,12},{12,16},{16,20},{20,24},{24,28},{28,32},{32,36}... | collective-permute-start | bytes 1572872 | tf_op jit(solution)/shard_map/while/body/eval_jaxpr/ppermute | solution.py:14
  322.3 12.6 %collective-permute-start = (f32[128,1024]{1,0:T(8,128)S(1)}, f32[128,1024]{1,0:T(8,128)S(1)}, u32[]{:S(2)}, u32[]{:S(2)}) collective-permute-start(f32[128,1024]{1,0:T(8,128)S(1)} %multiply_add_fusion.2), channel_id=1, source_target_pairs={{0,4},{4,8},{8,12},{12,16},{16,20},{20,24},{24,28},{28,32},{32,36}... | collective-permute-start | bytes 1572872 | tf_op jit(solution)/shard_map/while/body/eval_jaxpr/ppermute | solution.py:14
  335.0 12.6 %collective-permute-start = (f32[128,1024]{1,0:T(8,128)S(1)}, f32[128,1024]{1,0:T(8,128)S(1)}, u32[]{:S(2)}, u32[]{:S(2)}) collective-permute-start(f32[128,1024]{1,0:T(8,128)S(1)} %multiply_add_fusion.2), channel_id=1, source_target_pairs={{0,4},{4,8},{8,12},{12,16},{16,20},{20,24},{24,28},{28,32},{32,36}... | collective-permute-start | bytes 1572872 | tf_op jit(solution)/shard_map/while/body/eval_jaxpr/ppermute | solution.py:14
  347.7 12.6 %collective-permute-start = (f32[128,1024]{1,0:T(8,128)S(1)}, f32[128,1024]{1,0:T(8,128)S(1)}, u32[]{:S(2)}, u32[]{:S(2)}) collective-permute-start(f32[128,1024]{1,0:T(8,128)S(1)} %multiply_add_fusion.2), channel_id=1, source_target_pairs={{0,4},{4,8},{8,12},{12,16},{16,20},{20,24},{24,28},{28,32},{32,36}... | collective-permute-start | bytes 1572872 | tf_op jit(solution)/shard_map/while/body/eval_jaxpr/ppermute | solution.py:14
  360.4 12.6 %collective-permute-start = (f32[128,1024]{1,0:T(8,128)S(1)}, f32[128,1024]{1,0:T(8,128)S(1)}, u32[]{:S(2)}, u32[]{:S(2)}) collective-permute-start(f32[128,1024]{1,0:T(8,128)S(1)} %multiply_add_fusion.2), channel_id=1, source_target_pairs={{0,4},{4,8},{8,12},{12,16},{16,20},{20,24},{24,28},{28,32},{32,36}... | collective-permute-start | bytes 1572872 | tf_op jit(solution)/shard_map/while/body/eval_jaxpr/ppermute | solution.py:14
  373.0 12.6 %collective-permute-start = (f32[128,1024]{1,0:T(8,128)S(1)}, f32[128,1024]{1,0:T(8,128)S(1)}, u32[]{:S(2)}, u32[]{:S(2)}) collective-permute-start(f32[128,1024]{1,0:T(8,128)S(1)} %multiply_add_fusion.2), channel_id=1, source_target_pairs={{0,4},{4,8},{8,12},{12,16},{16,20},{20,24},{24,28},{28,32},{32,36}... | collective-permute-start | bytes 1572872 | tf_op jit(solution)/shard_map/while/body/eval_jaxpr/ppermute | solution.py:14
  385.7 12.6 %collective-permute-start = (f32[128,1024]{1,0:T(8,128)S(1)}, f32[128,1024]{1,0:T(8,128)S(1)}, u32[]{:S(2)}, u32[]{:S(2)}) collective-permute-start(f32[128,1024]{1,0:T(8,128)S(1)} %multiply_add_fusion.2), channel_id=1, source_target_pairs={{0,4},{4,8},{8,12},{12,16},{16,20},{20,24},{24,28},{28,32},{32,36}... | collective-permute-start | bytes 1572872 | tf_op jit(solution)/shard_map/while/body/eval_jaxpr/ppermute | solution.py:14
  (7 other events, 169.8 us)
Sparse Core Ops, SparseCore 0:
  9.5 67.0 all-gather.1
  434.8 122.1 reduce-scatter.1
where the time goes:
time: 569 us; the launch traced here: 568 us
  waiting for transfers between devices  325 us (57%)
  starting transfers between devices  159 us (28%)
  matrix products  26 us (5%)
  local copies, waits for them, and re-layouts  25.4 us (4%)
  other arithmetic  18.6 us (3%)
  between operations  13.5 us (2%)
    ppermute x31, waiting for transfers between devices, from_behind(): return lax.ppermute(block, axis, route)  202 us
    ppermute x31, starting transfers between devices, from_behind(): return lax.ppermute(block, axis, route)  159 us
    reduce_scatter x1, waiting for transfers between devices, per_device(): lax.psum_scatter(projected.astype(jnp.bfloat16), ('segment', 'mp'), scatt...  122 us
    dot_general x1, matrix products, per_device(): jnp.dot(normed, lax.all_gather(out_weight, 'ctx', axis=1, tiled=True), pr...  15.9 us
  transfers between devices with their start and end apart: 33, of which 32 were waited for; matrix products, arithmetic and copies ran while one was open for 9% of the time, Pallas kernels for 0%

commit v1 on v0

v1 whole, which is shorter than its diff:
```python
import jax
import jax.numpy as jnp
from jax import lax
from jax.experimental import pallas as pl
from jax.experimental.pallas import tpu as pltpu
from jax.sharding import PartitionSpec as P

HEAD_DIM = 64
STATE = 128
SPAN = 256
HEADS = 16
FEATS = HEADS * HEAD_DIM
TOKENS = 1024
SPANS = TOKENS // SPAN
HALF = FEATS // 2
MESH = pl.DeviceIdType.MESH
F32, BF16 = jnp.float32, jnp.bfloat16
ALL = slice(None)

PART_X = ((1, 2, 0), 256, 384)
PART_Y = ((2, 0, 1), 640, 384)
PART_Z = ((0, 1, 2), 0, 256)
PARTS = (PART_X, PART_Y, PART_Z)


def place():
    ctx = lax.axis_index("ctx")
    z = lax.axis_index("segment") * 2 + lax.axis_index("mp")
    return lax.div(ctx, 8), lax.rem(lax.div(ctx, 2), 4), z, lax.rem(ctx, 2)


def device(x, y, z, c):
    return {"ctx": (x * 4 + y) * 2 + c, "segment": lax.div(z, 2), "mp": lax.rem(z, 2)}


def around(value, distance):
    return lax.rem(value + distance, 4)


def shifted(pos, axis, distance):
    moved = list(pos)
    moved[axis] = around(moved[axis], distance)
    return device(*moved)


def dot(a, b, contract=((1,), (0,))):
    return lax.dot_general(a, b, (contract, ((), ())), preferred_element_type=F32)


def split3(v):
    hi = v.astype(BF16)
    rest = v - hi.astype(F32)
    mid = rest.astype(BF16)
    return hi, mid, (rest - mid.astype(F32)).astype(BF16)


class RingGather:
    def __init__(self, W, pos, index, axis, first, count, send, recv, sent):
        self.W, self.pos, self.index, self.axis = W, pos, index, axis
        self.first, self.count, self.send, self.recv, self.sent = first, count, send, recv, sent
        me = pos[axis]
        self.me, self.left, self.right, self.far = me, around(me, 3), around(me, 1), around(me, 2)

    def copy(self, who, half, distance, k):
        index = list(self.index)
        index[self.axis] = who
        first, count = self.first, self.count
        if half is not None:
            count = count // 2
            first = first + half * count
        ref = self.W.at[tuple(index) + (pl.ds(first, count), ALL)]
        return pltpu.make_async_remote_copy(
            src_ref=ref, dst_ref=ref, send_sem=self.send(k), recv_sem=self.recv(k),
            device_id=shifted(self.pos, self.axis, distance), device_id_type=MESH,
        )

    def start(self):
        for distance, k in ((1, 0), (3, 1)):
            c = self.copy(self.me, None, distance, k)
            c.start()
            self.sent.append(c)

    def forward(self):
        self.copy(self.left, None, 1, 0).wait_recv()
        a = self.copy(self.left, 0, 1, 2)
        a.start()
        self.copy(self.right, None, 3, 1).wait_recv()
        b = self.copy(self.right, 1, 3, 3)
        b.start()
        self.sent.extend([a, b])

    def finish(self):
        self.copy(self.far, 0, 1, 2).wait_recv()
        self.copy(self.far, 1, 3, 3).wait_recv()


def kernel(
    x_ref, gate_ref, b_ref, c_ref, ld_ref, gain_ref, w_ref, res_ref, o_ref,
    W, X, G, B, C, LD, RES, cum_s, cum_t, ecx, within, ent, thr, NB, ACT, ACC,
    sib_out, sib_in, sib_d, row_t, row_d, col_t, col_d, inc_out, inc, part_out, part_in,
    load_sem, s1, r1, s2, r2, s3, r3, sx, rx, sa, ra, sf, rf, sp, rp, out_sem,
):
    pos = place()
    x, y, z, c = pos
    sibling = device(x, y, z, 1 - c)
    sent = []

    loads = []
    for i, (src, dst) in enumerate((
        (ld_ref, LD), (w_ref, W.at[x, y, z]), (x_ref, X), (b_ref, B), (c_ref, C), (gate_ref, G), (res_ref, RES),
    )):
        loads.append(pltpu.make_async_copy(src, dst, load_sem.at[i]))
        loads[-1].start()

    barrier = pltpu.get_barrier_semaphore()
    partners = [sibling] + [shifted(pos, a, d) for a in range(3) for d in (1, 3, 2)]
    for p in partners:
        pl.semaphore_signal(barrier, inc=1, device_id=p, device_id_type=MESH)

    def push(src, dst, send, recv, target):
        cp = pltpu.make_async_remote_copy(
            src_ref=src, dst_ref=dst, send_sem=send, recv_sem=recv, device_id=target, device_id_type=MESH
        )
        cp.start()
        sent.append(cp)

    def arrived(dst, send, recv):
        pltpu.make_async_remote_copy(
            src_ref=dst, dst_ref=dst, send_sem=send, recv_sem=recv, device_id=sibling, device_id_type=MESH
        ).wait_recv()

    def sems(array, *at):
        return lambda k: array.at[(*at, k)]

    ph1, ph2, ph3 = [], [], []
    for q, ((a1, a2, a3), first, count) in enumerate(PARTS):
        ph1.append(RingGather(W, pos, list(pos[:3]), a1, first, count, sems(s1, q), sems(r1, q), sent))
        index = list(pos[:3])
        index[a1] = ALL
        ph2.append(RingGather(W, pos, index, a2, first, count, sems(s2, q), sems(r2, q), sent))
        subs = []
        for j, d in enumerate((0, 3, 1, 2)):
            index = list(pos[:3])
            index[a1] = ALL
            index[a2] = around(pos[a2], d)
            subs.append(RingGather(W, pos, index, a3, first, count, sems(s3, q, j), sems(r3, q, j), sent))
        ph3.append(subs)

    tri_r = lax.broadcasted_iota(jnp.int32, (SPAN, SPAN), 0)
    tri_c = lax.broadcasted_iota(jnp.int32, (SPAN, SPAN), 1)
    lower = tri_r >= tri_c
    tri = jnp.where(lower, 1.0, 0.0).astype(BF16)
    head_of = lax.div(lax.broadcasted_iota(jnp.int32, (2 * HEADS, FEATS), 1), HEAD_DIM)
    head_at = lax.rem(lax.broadcasted_iota(jnp.int32, (2 * HEADS, FEATS), 0), HEADS)
    spread = jnp.where(head_of == head_at, 1.0, 0.0).astype(BF16)

    def expand(v):
        hi = v.astype(BF16)
        lo = (v - hi.astype(F32)).astype(BF16)
        return dot(jnp.concatenate([hi, lo], axis=1), spread)

    loads[0].wait()
    for s in range(SPANS):
        hi, mid, lo = split3(LD[s * SPAN:(s + 1) * SPAN, :])
        cum = dot(tri, hi) + dot(tri, mid) + dot(tri, lo)
        cum_s[s] = cum
        cum_t[s] = cum.T
    loads[1].wait()
    pl.semaphore_wait(barrier, len(partners))
    for g in ph1:
        g.start()

    ent[0] = jnp.zeros((STATE, FEATS), F32)
    thr[0] = jnp.ones((8, FEATS), F32)
    for i in (2, 3):
        loads[i].wait()

    def fresh(s):
        rows = slice(s * SPAN, (s + 1) * SPAN)
        cum = cum_s[s]
        weights = expand(jnp.exp(cum[SPAN - 1:, :] - cum))
        weighted = (X[rows, :].astype(F32) * weights).astype(BF16)
        new = dot(B[rows, :], weighted, ((0,), (0,)))
        ecx[s] = expand(jnp.exp(cum))
        decay = ecx[s, SPAN - 1:, :]
        ent[s + 1] = decay * ent[s] + new
        thr[s + 1] = thr[s] * decay

    fresh(0)
    fresh(1)
    for g in ph1:
        g.forward()
    fresh(2)
    fresh(3)
    for g in ph1:
        g.finish()
    for g in ph2:
        g.start()
    for t in ph3:
        t[0].start()

    mine = pl.ds(pl.multiple_of(c * HALF, HALF), HALF)
    other = pl.ds(pl.multiple_of((1 - c) * HALF, HALF), HALF)

    sib_out[...] = ent[SPANS, :, other].astype(BF16)
    push(sib_out, sib_in, sx.at[0], rx.at[0], sibling)
    push(thr.at[SPANS], sib_d, sx.at[1], rx.at[1], sibling)

    for i in (4,):
        loads[i].wait()

    lane_low = lax.broadcasted_iota(jnp.int32, (128, 128), 1) < HEAD_DIM

    def within_span(s):
        rows = slice(s * SPAN, (s + 1) * SPAN)
        scores = dot(C[rows, :], B[rows, :], ((1,), (1,)))
        scores = jnp.where(lower, scores, 0.0)
        top, bottom = scores[:128, :128], scores[128:, :]
        cum, cum_row = cum_s[s], cum_t[s]
        for pair in range(HEADS // 2):
            lanes = slice(pair * 128, (pair + 1) * 128)
            xs = X[rows, lanes]
            tops, bottoms = [], []
            for h in (2 * pair, 2 * pair + 1):
                col, row = cum[:, h:h + 1], cum_row[h:h + 1, :]
                mix = (jnp.exp(jnp.minimum(col[:128] - row[:, :128], 0.0)) * top).astype(BF16)
                tops.append(dot(mix, xs[:128]))
                mix = (jnp.exp(jnp.minimum(col[128:] - row, 0.0)) * bottom).astype(BF16)
                bottoms.append(dot(mix, xs))
            within[s, :128, lanes] = jnp.where(lane_low, tops[0], tops[1])
            within[s, 128:, lanes] = jnp.where(lane_low, bottoms[0], bottoms[1])

    within_span(0)

    arrived(sib_in, sx.at[0], rx.at[0])
    arrived(sib_d, sx.at[1], rx.at[1])
    first_core = c == 0
    own_state, own_decay = ent[SPANS, :, mine], thr[SPANS, 0:1, mine]
    sib_state, sib_decay = sib_in[...].astype(F32), sib_d[0:1, mine]
    state0 = jnp.where(first_core, own_state, sib_state)
    state1 = jnp.where(first_core, sib_state, own_state)
    decay0 = jnp.where(first_core, own_decay, sib_decay)
    decay1 = jnp.where(first_core, sib_decay, own_decay)

    def exchange(states, decays, axis, state, decay, at):
        me = pos[axis]
        states[me] = state.astype(BF16)
        decays[me] = jnp.broadcast_to(decay, (8, HALF))
        for i, d in enumerate((1, 3, 2)):
            target = shifted(pos, axis, d)
            push(states.at[me], states.at[me], sx.at[at + i], rx.at[at + i], target)
            push(decays.at[me], decays.at[me], sx.at[at + 3 + i], rx.at[at + 3 + i], target)

    def combine(states, decays, axis, at):
        me = pos[axis]
        for i, d in enumerate((3, 1, 2)):
            who = around(me, d)
            arrived(states.at[who], sx.at[at + i], rx.at[at + i])
            arrived(decays.at[who], sx.at[at + 3 + i], rx.at[at + 3 + i])
        before = jnp.zeros((STATE, HALF), F32)
        through = jnp.ones((1, HALF), F32)
        total, total_decay = before, through
        for t in range(4):
            state, decay = states[t].astype(F32), decays[t, 0:1, :]
            before = jnp.where(t < me, decay * before + state, before)
            through = jnp.where(t < me, through * decay, through)
            total = decay * total + state
            total_decay = total_decay * decay
        return before, through, total, total_decay

    exchange(row_t, row_d, 1, decay1 * state0 + state1, decay0 * decay1, 2)
    for g, t in zip(ph2, ph3):
        g.forward()
        t[1].start()
        t[2].start()

    within_span(1)

    before_y, through_y, total, total_decay = combine(row_t, row_d, 1, 2)
    exchange(col_t, col_d, 0, total, total_decay, 8)
    for g, t in zip(ph2, ph3):
        g.finish()
        t[3].start()

    within_span(2)

    before_x, _, _, _ = combine(col_t, col_d, 0, 8)
    enter0 = through_y * before_x + before_y
    enter1 = decay0 * enter0 + state0
    inc[c] = jnp.where(first_core, enter0, enter1).astype(BF16)
    inc_out[...] = jnp.where(first_core, enter1, enter0).astype(BF16)
    push(inc_out, inc.at[c], sx.at[14], rx.at[14], sibling)

    within_span(3)

    for i in (5, 6):
        loads[i].wait()
    arrived(inc.at[1 - c], sx.at[14], rx.at[14])

    def normed(q):
        rows = pl.ds(pl.multiple_of(q * SPAN, SPAN), SPAN)
        incoming = jnp.concatenate([inc[0], inc[1]], axis=1).astype(F32)
        state = (ent[q] + thr[q, 0:1, :] * incoming).astype(BF16)
        mixed = within[q] + dot(C[rows, :], state) * ecx[q]
        g = G[rows, :].astype(F32)
        gated = mixed * (g / (1.0 + jnp.exp(-g)))
        factor = lax.rsqrt(jnp.mean(gated * gated, axis=1, keepdims=True) + 1e-05)
        return (gated * factor * gain_ref[...]).astype(BF16)

    for i in (1, 2, 3):
        q = around(z, i)
        NB[i - 1] = normed(q)
        push(NB.at[i - 1], ACT.at[c, z], sa.at[i - 1], ra.at[i - 1], device(x, y, q, c))
    ACT[c, z] = normed(z)
    push(ACT.at[c, z], ACT.at[c, z], sf.at[0], rf.at[0], sibling)

    for t in ph3:
        t[0].forward()
    ACC[...] = jnp.zeros(ACC.shape, F32)

    for i in (1, 3, 2):
        who = around(z, 4 - i)
        arrived(ACT.at[c, who], sa.at[i - 1], ra.at[i - 1])
        push(ACT.at[c, who], ACT.at[c, who], sf.at[i], rf.at[i], sibling)
    for j in (1, 2, 3):
        for t in ph3:
            t[j].forward()
    for i in range(4):
        arrived(ACT.at[1 - c, around(z, 4 - i)], sf.at[i], rf.at[i])

    def multiply(b0, b1, zs, first, count):
        total = None
        for zz in zs:
            lhs = ACT[:, zz, :, first:first + count].reshape(2 * SPAN, count)
            rhs = jnp.concatenate(
                [W[b0[0], b0[1], zz, first:first + count, :], W[b1[0], b1[1], zz, first:first + count, :]], axis=1
            )
            d = dot(lhs, rhs)
            total = d if total is None else total + d
        ACC[b0[0], b0[1]] += total[:, :128]
        ACC[b1[0], b1[1]] += total[:, 128:]

    def over_x(first_step, steps):
        _, first, count = PART_X

        @pl.loop(0, 2 * steps)
        def _(i):
            xx = around(x, 3 + first_step + lax.div(i, 2))
            yy = lax.rem(i, 2) * 2
            multiply((xx, yy), (xx, yy + 1), range(4), first, count)

    def over_y(first_step, steps):
        _, first, count = PART_Y

        @pl.loop(0, 2 * steps)
        def _(i):
            yy = around(y, 3 + first_step + lax.div(i, 2))
            xx = lax.rem(i, 2) * 2
            multiply((xx, yy), (xx + 1, yy), range(4), first, count)

    def over_z(distances):
        _, first, count = PART_Z

        @pl.loop(0, 8)
        def _(i):
            xx, yy = lax.div(i, 2), lax.rem(i, 2) * 2
            multiply((xx, yy), (xx, yy + 1), [around(z, d) for d in distances], first, count)

    over_x(0, 3)
    over_y(0, 3)
    over_z((3, 0, 1))
    for q, stage in ((0, lambda: over_x(3, 1)), (1, lambda: over_y(3, 1)), (2, lambda: over_z((2,)))):
        for j in range(4):
            ph3[q][j].finish()
        stage()

    for xx in range(4):
        for yy in range(4):
            rows = pl.ds(pl.multiple_of((1 - c) * SPAN, SPAN), SPAN)
            part_out[xx, yy] = ACC[xx, yy, rows, :].astype(BF16)
        push(part_out.at[xx], part_in.at[xx], sp.at[xx], rp.at[xx], sibling)
    outs = []
    for xx in range(4):
        rows = pl.ds(pl.multiple_of(c * SPAN, SPAN), SPAN)
        for yy in range(4):
            lanes = pl.ds(pl.multiple_of((xx * 8 + yy * 2 + c) * 128, 128), 128)
            RES[:, lanes] = (RES[:, lanes].astype(F32) + ACC[xx, yy, rows, :]).astype(BF16)
        arrived(part_in.at[xx], sp.at[xx], rp.at[xx])
        for yy in range(4):
            lanes = pl.ds(pl.multiple_of((xx * 8 + yy * 2 + 1 - c) * 128, 128), 128)
            RES[:, lanes] = (RES[:, lanes].astype(F32) + part_in[xx, yy].astype(F32)).astype(BF16)
        cols = pl.ds(xx * 1024, 1024)
        outs.append(pltpu.make_async_copy(RES.at[:, cols], o_ref.at[:, cols], out_sem.at[xx]))
        outs[-1].start()
    for cp in outs:
        cp.wait()
    for cp in sent:
        cp.wait_send()


def per_device(
    head_inputs, gate_input, state_write, state_read, log_decay, norm_gain, out_weight, residual
):
    any_space = pl.BlockSpec(memory_space=pl.ANY)
    vmem, dma = pltpu.VMEM, pltpu.SemaphoreType.DMA
    return pl.pallas_call(
        kernel,
        out_shape=jax.ShapeDtypeStruct(residual.shape, BF16),
        in_specs=[any_space] * 5 + [pl.BlockSpec(memory_space=pltpu.VMEM)] + [any_space] * 2,
        out_specs=any_space,
        scratch_shapes=[
            vmem((4, 4, 4, 1024, 128), BF16),
            vmem((TOKENS, FEATS), BF16),
            vmem((TOKENS, FEATS), BF16),
            vmem((TOKENS, STATE), BF16),
            vmem((TOKENS, STATE), BF16),
            vmem((TOKENS, HEADS), F32),
            vmem((SPAN, 4096), BF16),
            vmem((SPANS, SPAN, HEADS), F32),
            vmem((SPANS, HEADS, SPAN), F32),
            vmem((SPANS, SPAN, FEATS), F32),
            vmem((SPANS, SPAN, FEATS), F32),
            vmem((SPANS + 1, STATE, FEATS), F32),
            vmem((SPANS + 1, 8, FEATS), F32),
            vmem((3, SPAN, FEATS), BF16),
            vmem((2, 4, SPAN, FEATS), BF16),
            vmem((4, 4, 2 * SPAN, 128), F32),
            vmem((STATE, HALF), BF16),
            vmem((STATE, HALF), BF16),
            vmem((8, FEATS), F32),
            vmem((4, STATE, HALF), BF16),
            vmem((4, 8, HALF), F32),
            vmem((4, STATE, HALF), BF16),
            vmem((4, 8, HALF), F32),
            vmem((STATE, HALF), BF16),
            vmem((2, STATE, HALF), BF16),
            vmem((4, 4, SPAN, 128), BF16),
            vmem((4, 4, SPAN, 128), BF16),
            dma((7,)),
            dma((3, 4)), dma((3, 4)), dma((3, 4)), dma((3, 4)), dma((3, 4, 4)), dma((3, 4, 4)),
            dma((15,)), dma((15,)),
            dma((3,)), dma((3,)),
            dma((4,)), dma((4,)),
            dma((4,)), dma((4,)),
            dma((4,)),
        ],
        compiler_params=pltpu.CompilerParams(
            collective_id=0, has_side_effects=True, vmem_limit_bytes=60 << 20
        ),
        cost_estimate=pl.CostEstimate(flops=11 * 10**9, bytes_accessed=12 << 20, transcendentals=4 << 20),
        name="spanned_mixer",
    )(head_inputs, gate_input, state_write, state_read, log_decay, norm_gain.reshape(1, -1), out_weight, residual)


def solution(mesh):
    placed = (
        P("ctx", ("segment", "mp")),
        P("ctx", ("segment", "mp")),
        P("ctx", ("segment", "mp")),
        P("ctx", ("segment", "mp")),
        P("ctx", ("segment", "mp")),
        P(("segment", "mp")),
        P(("segment", "mp"), "ctx"),
        P(("ctx", "segment", "mp"), None),
    )
    return jax.shard_map(
        per_device,
        mesh=mesh,
        in_specs=placed,
        out_specs=P(("ctx", "segment", "mp"), None),
        check_vma=False,
    )
```

time: 569 us -> 122 us (0.21)
  waiting for transfers between devices: 325 us -> 0 us
  starting transfers between devices: 159 us -> 0 us
  Pallas kernels: 0 us -> 116 us
  matrix products: 26 us -> 0 us
  local copies, waits for them, and re-layouts: 25.4 us -> 4.97 us
  other arithmetic: 18.6 us -> 0 us
  between operations: 13.5 us -> 0.01 us
    ppermute x31 -> x0, waiting for transfers between devices: 202 us -> none  [from_behind(): return lax.ppermute(block, axis, route)]
    ppermute x31 -> x0, starting transfers between devices: 159 us -> none  [from_behind(): return lax.ppermute(block, axis, route)]
    reduce_scatter x1 -> x0, waiting for transfers between devices: 122 us -> none  [per_device(): lax.psum_scatter(projected.astype(jnp.bfloat16), ('segment', 'mp'), scatt...]
    pallas_call x0 -> x1, Pallas kernels: none -> 116 us  [per_device(): pl.pallas_call(kernel, out_shape=jax.ShapeDtypeStruct(residual.shape, BF1...]
    dot_general x5 -> x0, matrix products: 26 us -> none  [the longest x1 15.9 us: per_device(): jnp.dot(normed, lax.all_gather(out_weight, 'ctx', axis=1, tiled=True), pr...]
    reshape x3 -> x0, local copies, waits for them, and re-layouts: 7.36 us -> none  [the longest x1 6.41 us: per_device(): head_rows = head_inputs.reshape(spans, SPAN, heads_here, HEAD_DIM)]
    convert_element_type x2 -> x0, other arithmetic: 6.35 us -> none  [the longest x1 3.69 us: per_device(): return (residual.astype(jnp.float32) + summed).astype(jnp.bfloat16)]
  transfers between devices with their start and end apart: 33 -> 0, of which waited for: 32 -> 0; matrix products, arithmetic and copies ran while one was open for 9% -> 0% of each run, Pallas kernels for 0% -> 0%
where the time goes in v1:
time: 122 us; the launch traced here: 121 us
  Pallas kernels  116 us (95%)
  local copies, waits for them, and re-layouts  4.97 us (4%)
    pallas_call x1, Pallas kernels, per_device(): pl.pallas_call(kernel, out_shape=jax.ShapeDtypeStruct(residual.shape, BF1...  116 us
    unnamed x2, local copies, waits for them, and re-layouts  4.97 us

profile of v1, /device:TPU:1, one launch (start us, length us, event | category | flops | bytes accessed | tf_op | source)
XLA Modules:
  0.0 121.3 jit_solution(1341965158706358969)
XLA Ops:
  0.0 1.8 %copy.9.ld_ref = f32[1024,16]{1,0:T(8,128)} copy(f32[1024,16]{0,1:T(8,128)} %param.12) | data formatting | bytes 131072 | tf_op args[4]
  1.8 116.3 %spanned_mixer.1 = bf16[256,4096]{1,0:T(8,128)(2,1)} custom-call(bf16[1024,1024]{1,0:T(8,128)(2,1)} %x_ref.1, bf16[1024,1024]{1,0:T(8,128)(2,1)} %gate_ref.1, bf16[1024,128]{1,0:T(8,128)(2,1)} %b_ref.1, bf16[1024,128]{1,0:T(8,128)(2,1)} %c_ref.1, f32[1024,16]{1,0:T(8,128)} %copy.9.ld_ref, f32[1,1024]{1,0:T(1,128)} %bitcast.1, bf16[1024,128]{1,0:T(8,128)(2,1)} %w_ref.1, ...), custom_call_target="tpu_custom_call" | custom-call | flops 11000000512 | bytes 12582912 | tf_op jit(solution)/shard_map/spanned_mixer/pallas_call | solution.py:406
  118.2 3.1 %copy.11 = bf16[256,4096]{1,0:T(8,128)(2,1)} copy(bf16[256,4096]{1,0:T(8,128)(2,1)} %spanned_mixer.1) | data formatting | bytes 4194304

commit v2 on v1

v2 whole, which is shorter than its diff:
```python
import jax
import jax.numpy as jnp
from jax import lax
from jax.experimental import pallas as pl
from jax.experimental.pallas import tpu as pltpu
from jax.sharding import PartitionSpec as P

HEAD_DIM = 64
STATE = 128
SPAN = 256
HEADS = 16
FEATS = HEADS * HEAD_DIM
TOKENS = 1024
SPANS = TOKENS // SPAN
HALF = FEATS // 2
MESSAGE = STATE + 16
MESH = pl.DeviceIdType.MESH
F32, BF16 = jnp.float32, jnp.bfloat16
ALL = slice(None)

def place():
    ctx = lax.axis_index("ctx")
    z = lax.axis_index("segment") * 2 + lax.axis_index("mp")
    return lax.div(ctx, 8), lax.rem(lax.div(ctx, 2), 4), z, lax.rem(ctx, 2)


def device(x, y, z, c):
    return {"ctx": (x * 4 + y) * 2 + c, "segment": lax.div(z, 2), "mp": lax.rem(z, 2)}


def around(value, distance):
    return lax.rem(value + distance, 4)


def shifted(pos, axis, distance):
    moved = list(pos)
    moved[axis] = around(moved[axis], distance)
    return device(*moved)


def dot(a, b, contract=((1,), (0,))):
    return lax.dot_general(a, b, (contract, ((), ())), preferred_element_type=F32)


def split3(v):
    hi = v.astype(BF16)
    rest = v - hi.astype(F32)
    mid = rest.astype(BF16)
    return hi, mid, (rest - mid.astype(F32)).astype(BF16)


class RingGather:
    def __init__(self, W, pos, index, axis, send, recv, sent):
        self.W, self.pos, self.index, self.axis = W, pos, index, axis
        self.send, self.recv, self.sent = send, recv, sent
        me = pos[axis]
        self.me, self.left, self.right, self.far = me, around(me, 3), around(me, 1), around(me, 2)

    def copy(self, who, half, distance, k):
        index = list(self.index)
        index[self.axis] = who
        first, count = (0, 1024) if half is None else (512 * half, 512)
        ref = self.W.at[tuple(index) + (pl.ds(first, count), ALL)]
        return pltpu.make_async_remote_copy(
            src_ref=ref, dst_ref=ref, send_sem=self.send(k), recv_sem=self.recv(k),
            device_id=shifted(self.pos, self.axis, distance), device_id_type=MESH,
        )

    def start(self):
        for distance, k in ((1, 0), (3, 1)):
            c = self.copy(self.me, None, distance, k)
            c.start()
            self.sent.append(c)

    def forward(self):
        self.copy(self.left, None, 1, 0).wait_recv()
        a = self.copy(self.left, 0, 1, 2)
        a.start()
        self.copy(self.right, None, 3, 1).wait_recv()
        b = self.copy(self.right, 1, 3, 3)
        b.start()
        self.sent.extend([a, b])

    def finish(self):
        self.copy(self.far, 0, 1, 2).wait_recv()
        self.copy(self.far, 1, 3, 3).wait_recv()


def kernel(
    x_ref, gate_ref, b_ref, c_ref, ld_ref, gain_ref, w_ref, kept_ref, got_ref,
    W, X, G, B, C, LD, cum_s, cum_t, ecx, within, ent, thr, NB, ACT, away, keep,
    sib_out, sib_in, row_out, row_in, col, back_out, back_in, inc_out, inc,
    load_sem, s0, r0, s1, r1, s2, r2, sx, rx, sa, ra, sf, rf, sr, rr, sk, rk, out_sem,
):
    pos = place()
    x, y, z, c = pos
    sibling = device(x, y, z, 1 - c)
    sent = []

    loads = []
    for i, (src, dst) in enumerate((
        (ld_ref, LD), (w_ref, W.at[x, y, 0]), (x_ref, X), (b_ref, B), (c_ref, C), (gate_ref, G),
    )):
        loads.append(pltpu.make_async_copy(src, dst, load_sem.at[i]))
        loads[-1].start()

    barrier = pltpu.get_barrier_semaphore()
    even = 1 - lax.rem(z, 2)
    za, zb = around(z, 3 - 2 * even), around(z, 1 + 2 * even)
    zo = around(z, 2)
    partners = [sibling] + [shifted(pos, a, d) for a in range(2) for d in (1, 3, 2)]
    partners += [device(x, y, zz, cc) for zz in (za, zb) for cc in (0, 1)]
    for p in partners:
        pl.semaphore_signal(barrier, inc=1, device_id=p, device_id_type=MESH)

    def push(src, dst, send, recv, target):
        cp = pltpu.make_async_remote_copy(
            src_ref=src, dst_ref=dst, send_sem=send, recv_sem=recv, device_id=target, device_id_type=MESH
        )
        cp.start()
        sent.append(cp)

    def arrived(dst, send, recv):
        pltpu.make_async_remote_copy(
            src_ref=dst, dst_ref=dst, send_sem=send, recv_sem=recv, device_id=sibling, device_id_type=MESH
        ).wait_recv()

    def sems(array, *at):
        return lambda k: array.at[(*at, k)]

    ph1, ph2 = [], []
    for slot, (a1, a2) in enumerate(((1, 0), (0, 1))):
        ph1.append(RingGather(W, pos, [x, y, slot], a1, sems(s1, slot), sems(r1, slot), sent))
        subs = []
        for j, d in enumerate((0, 3, 1, 2)):
            index = [x, y, slot]
            index[a1] = around(pos[a1], d)
            subs.append(RingGather(W, pos, index, a2, sems(s2, slot, j), sems(r2, slot, j), sent))
        ph2.append(subs)

    tri_r = lax.broadcasted_iota(jnp.int32, (SPAN, SPAN), 0)
    tri_c = lax.broadcasted_iota(jnp.int32, (SPAN, SPAN), 1)
    lower = tri_r >= tri_c
    tri = jnp.where(tri_r <= tri_c, 1.0, 0.0).astype(BF16)
    head_of = lax.div(lax.broadcasted_iota(jnp.int32, (2 * HEADS, FEATS), 1), HEAD_DIM)
    head_at = lax.rem(lax.broadcasted_iota(jnp.int32, (2 * HEADS, FEATS), 0), HEADS)
    spread = jnp.where(head_of == head_at, 1.0, 0.0).astype(BF16)

    def expand(v):
        hi = v.astype(BF16)
        lo = (v - hi.astype(F32)).astype(BF16)
        return dot(jnp.concatenate([hi, lo], axis=1), spread)

    loads[0].wait()
    for s in range(SPANS):
        hi, mid, lo = split3(LD[:, s * SPAN:(s + 1) * SPAN])
        cum = dot(hi, tri) + dot(mid, tri) + dot(lo, tri)
        cum_t[s] = cum
        cum_s[s] = cum.T
    loads[1].wait()
    pl.semaphore_wait(barrier, len(partners))
    odd_y = lax.rem(y, 2)
    zp = around(z, (1 - odd_y) * (3 - 2 * even) + odd_y * (1 + 2 * even))
    push(W.at[x, y, 0], W.at[x, y, 1], s0, r0, device(x, y, zp, c))
    ph1[0].start()
    ph2[0][0].start()

    ent[0] = jnp.zeros((STATE, FEATS), F32)
    thr[0] = jnp.ones((8, FEATS), F32)
    for i in (2, 3):
        loads[i].wait()

    def fresh(s):
        rows = slice(s * SPAN, (s + 1) * SPAN)
        cum = cum_s[s]
        weights = expand(jnp.exp(cum[SPAN - 1:, :] - cum))
        weighted = (X[rows, :].astype(F32) * weights).astype(BF16)
        new = dot(B[rows, :], weighted, ((0,), (0,)))
        ecx[s] = expand(jnp.exp(cum))
        decay = ecx[s, SPAN - 1:, :]
        ent[s + 1] = decay * ent[s] + new
        thr[s + 1] = thr[s] * decay

    for s in range(SPANS):
        fresh(s)

    mine = pl.ds(pl.multiple_of(c * HALF, HALF), HALF)
    other = pl.ds(pl.multiple_of((1 - c) * HALF, HALF), HALF)

    def message(state, decay):
        hi = decay.astype(BF16)
        lo = (decay - hi.astype(F32)).astype(BF16)
        shape = (8, decay.shape[1])
        return state.astype(BF16), jnp.concatenate([jnp.broadcast_to(hi, shape), jnp.broadcast_to(lo, shape)], axis=0)

    def opened(block):
        return block[:STATE].astype(F32), block[STATE:STATE + 1].astype(F32) + block[STATE + 8:STATE + 9].astype(F32)

    sib_out[:STATE], sib_out[STATE:] = message(ent[SPANS, :, other], thr[SPANS, 0:1, other])
    push(sib_out, sib_in, sx.at[0], rx.at[0], sibling)

    for i in (4,):
        loads[i].wait()

    lane_low = lax.broadcasted_iota(jnp.int32, (128, 128), 1) < HEAD_DIM

    def within_span(s):
        rows = slice(s * SPAN, (s + 1) * SPAN)
        scores = dot(C[rows, :], B[rows, :], ((1,), (1,)))
        scores = jnp.where(lower, scores, 0.0)
        top, bottom = scores[:128, :128], scores[128:, :]
        cum, cum_row = cum_s[s], cum_t[s]
        for pair in range(HEADS // 2):
            lanes = slice(pair * 128, (pair + 1) * 128)
            xs = X[rows, lanes]
            tops, bottoms = [], []
            for h in (2 * pair, 2 * pair + 1):
                col, row = cum[:, h:h + 1], cum_row[h:h + 1, :]
                mix = (jnp.exp(jnp.minimum(col[:128] - row[:, :128], 0.0)) * top).astype(BF16)
                tops.append(dot(mix, xs[:128]))
                mix = (jnp.exp(jnp.minimum(col[128:] - row, 0.0)) * bottom).astype(BF16)
                bottoms.append(dot(mix, xs))
            within[s, :128, lanes] = jnp.where(lane_low, tops[0], tops[1])
            within[s, 128:, lanes] = jnp.where(lane_low, bottoms[0], bottoms[1])

    arrived(W.at[x, y, 1], s0, r0)
    ph1[1].start()
    ph2[1][0].start()

    arrived(sib_in, sx.at[0], rx.at[0])
    first_core = c == 0
    own_state, own_decay = ent[SPANS, :, mine], thr[SPANS, 0:1, mine]
    sib_state, sib_decay = opened(sib_in[...])
    state0 = jnp.where(first_core, own_state, sib_state)
    state1 = jnp.where(first_core, sib_state, own_state)
    decay0 = jnp.where(first_core, own_decay, sib_decay)
    decay1 = jnp.where(first_core, sib_decay, own_decay)
    chip_state, chip_decay = message(decay1 * state0 + state1, decay0 * decay1)
    for t in range(4):
        row_out[t, :STATE] = chip_state[:, t * 128:(t + 1) * 128]
        row_out[t, STATE:] = chip_decay[:, t * 128:(t + 1) * 128]
    for i in (2, 1, 3):
        to = around(y, i)
        push(row_out.at[to], row_in.at[y], sx.at[i], rx.at[i], shifted(pos, 1, i))
    row_in[y] = row_out[y]

    ph1[0].forward()
    ph2[0][1].start()
    ph2[0][2].start()

    within_span(0)

    for i in (1, 3, 2):
        arrived(row_in.at[around(y, 4 - i)], sx.at[i], rx.at[i])
    before_y, through_y = [jnp.zeros((STATE, 128), F32)], [jnp.ones((1, 128), F32)]
    for t in range(4):
        state, decay = opened(row_in[t])
        before_y.append(decay * before_y[t] + state)
        through_y.append(through_y[t] * decay)
    row_state, row_decay = message(before_y[4], through_y[4])
    col[x, :STATE] = row_state
    col[x, STATE:] = row_decay
    for i in (2, 1, 3):
        push(col.at[x], col.at[x], sx.at[3 + i], rx.at[3 + i], shifted(pos, 0, i))

    ph1[1].forward()
    ph2[1][1].start()
    ph2[1][2].start()
    ph1[0].finish()
    ph2[0][3].start()

    within_span(1)

    for i in (1, 3, 2):
        arrived(col.at[around(x, 4 - i)], sx.at[3 + i], rx.at[3 + i])
    before_x = jnp.zeros((STATE, 128), F32)
    for t in range(4):
        state, decay = opened(col[t])
        before_x = jnp.where(t < x, decay * before_x + state, before_x)
    for t in range(4):
        back_out[t] = (through_y[t] * before_x + before_y[t]).astype(BF16)
    for i in (2, 1, 3):
        to = around(y, i)
        push(back_out.at[to], back_in.at[y], sx.at[6 + i], rx.at[6 + i], shifted(pos, 1, i))
    back_in[y] = back_out[y]

    ph1[1].finish()
    ph2[1][3].start()

    within_span(2)

    for i in (1, 3, 2):
        arrived(back_in.at[around(y, 4 - i)], sx.at[6 + i], rx.at[6 + i])
    enter0 = jnp.concatenate([back_in[t] for t in range(4)], axis=1).astype(F32)
    enter1 = decay0 * enter0 + state0
    inc[c] = jnp.where(first_core, enter0, enter1).astype(BF16)
    inc_out[...] = jnp.where(first_core, enter1, enter0).astype(BF16)
    push(inc_out, inc.at[c], sx.at[10], rx.at[10], sibling)

    for t in ph2:
        t[0].forward()

    within_span(3)

    for i in (5,):
        loads[i].wait()
    arrived(inc.at[1 - c], sx.at[10], rx.at[10])

    def normed(q):
        rows = pl.ds(pl.multiple_of(q * SPAN, SPAN), SPAN)
        incoming = jnp.concatenate([inc[0], inc[1]], axis=1).astype(F32)
        state = (ent[q] + thr[q, 0:1, :] * incoming).astype(BF16)
        mixed = within[q] + dot(C[rows, :], state) * ecx[q]
        g = G[rows, :].astype(F32)
        gated = mixed * (g / (1.0 + jnp.exp(-g)))
        factor = lax.rsqrt(jnp.mean(gated * gated, axis=1, keepdims=True) + 1e-05)
        return (gated * factor * gain_ref[...]).astype(BF16)

    NB[...] = normed(zo)
    push(NB, ACT.at[3, c], sa.at[0], ra.at[0], device(x, y, za, c))
    push(NB, ACT.at[4, c], sa.at[1], ra.at[1], device(x, y, zb, c))
    ACT[1, c] = normed(za)
    push(ACT.at[1, c], ACT.at[5, c], sa.at[2], ra.at[2], device(x, y, za, c))
    ACT[2, c] = normed(zb)
    push(ACT.at[2, c], ACT.at[6, c], sa.at[3], ra.at[3], device(x, y, zb, c))

    def share(slot):
        push(ACT.at[slot, c], ACT.at[slot, c], sf.at[slot], rf.at[slot], sibling)

    share(1)
    share(2)
    ACT[0, c] = normed(z)
    share(0)

    for j in (1, 2, 3):
        for t in ph2:
            t[j].forward()

    for i in (0, 1):
        arrived(ACT.at[3 + i, c], sa.at[i], ra.at[i])
        share(3 + i)
    for slot in (1, 2, 3, 4):
        arrived(ACT.at[slot, 1 - c], sf.at[slot], rf.at[slot])

    def product(own, other, b0, b1):
        lhs = jnp.concatenate([ACT[own].reshape(2 * SPAN, FEATS), ACT[other].reshape(2 * SPAN, FEATS)], axis=1)
        rhs = jnp.concatenate([W[b[0], b[1]].reshape(2 * FEATS, 128) for b in (b0, b1)], axis=1)
        return dot(lhs, rhs).astype(BF16)

    def columns(bx, by, core):
        return pl.ds(pl.multiple_of((bx * 8 + by * 2 + core) * 128, 128), 128)

    def away_copy(bx, by, section):
        odd = lax.rem(by, 2)
        target = around(z, (1 - odd) * (1 + 2 * even) + odd * (3 - 2 * even))
        return pltpu.make_async_remote_copy(
            src_ref=away.at[bx, by, section], dst_ref=got_ref.at[:, columns(bx, by, c)],
            send_sem=sr.at[bx, by, section], recv_sem=rr.at[bx, by, c],
            device_id=device(x, y, target, section), device_id_type=MESH,
        )

    def keep_local(bx, by):
        return pltpu.make_async_copy(keep.at[bx, by, c], kept_ref.at[:, columns(bx, by, c)], out_sem.at[bx, by])

    def keep_remote(bx, by):
        return pltpu.make_async_remote_copy(
            src_ref=keep.at[bx, by, 1 - c], dst_ref=kept_ref.at[:, columns(bx, by, c)],
            send_sem=sk.at[bx, by], recv_sem=rk.at[bx, by], device_id=sibling, device_id_type=MESH,
        )

    near = (((0, 3), (0, 1)), ((3, 3), (3, 1)), ((1, 3), (1, 1)), ((0, 0), (3, 0)))
    rest = (((1, 0), (2, 0)), ((2, 3), (2, 1)), ((0, 2), (1, 2)), ((2, 2), (3, 2)))

    def over_pairs(table, body):
        @pl.loop(0, 4)
        def _(i):
            def pick(b, axis):
                value = table[0][b][axis]
                for k in (1, 2, 3):
                    value = jnp.where(i == k, table[k][b][axis], value)
                return around(pos[axis], value)

            body((pick(0, 0), pick(0, 1)), (pick(1, 0), pick(1, 1)))

    def send_away(b0, b1):
        odd = lax.rem(b0[1], 2)
        result = product(2 - odd, 3 + odd, b0, b1)
        for k, (bx, by) in enumerate((b0, b1)):
            for section in (0, 1):
                away[bx, by, section] = result[section * SPAN:(section + 1) * SPAN, k * 128:(k + 1) * 128]
                away_copy(bx, by, section).start()

    def keep_here(b0, b1):
        odd = lax.rem(b0[1], 2)
        result = product(0, 5 + odd, b0, b1)
        for k, (bx, by) in enumerate((b0, b1)):
            for section in (0, 1):
                keep[bx, by, section] = result[section * SPAN:(section + 1) * SPAN, k * 128:(k + 1) * 128]
            keep_remote(bx, by).start()
            keep_local(bx, by).start()

    over_pairs(near, send_away)
    for t in ph2:
        for j in range(4):
            t[j].finish()
    over_pairs(rest, send_away)
    for i in (2, 3):
        arrived(ACT.at[3 + i, c], sa.at[i], ra.at[i])
        share(3 + i)
    for slot in (0, 5, 6):
        arrived(ACT.at[slot, 1 - c], sf.at[slot], rf.at[slot])
    over_pairs(near, keep_here)
    over_pairs(rest, keep_here)

    @pl.loop(0, 16)
    def _(i):
        bx, by = lax.div(i, 4), lax.rem(i, 4)
        keep_local(bx, by).wait()
        keep_remote(bx, by).wait_send()
        arrived(kept_ref.at[:, columns(bx, by, 1 - c)], sk.at[bx, by], rk.at[bx, by])
        for section in (0, 1):
            away_copy(bx, by, section).wait_send()
        for core in (0, 1):
            arrived(got_ref.at[:, columns(bx, by, core)], sr.at[bx, by, core], rr.at[bx, by, core])

    for cp in sent:
        cp.wait_send()


def per_device(
    head_inputs, gate_input, state_write, state_read, log_decay, norm_gain, out_weight, residual
):
    any_space = pl.BlockSpec(memory_space=pl.ANY)
    vmem, dma = pltpu.VMEM, pltpu.SemaphoreType.DMA
    kept, got = pl.pallas_call(
        kernel,
        out_shape=[jax.ShapeDtypeStruct(residual.shape, BF16)] * 2,
        in_specs=[any_space] * 5 + [pl.BlockSpec(memory_space=pltpu.VMEM)] + [any_space],
        out_specs=[any_space] * 2,
        scratch_shapes=[
            vmem((4, 4, 2, 1024, 128), BF16),
            vmem((TOKENS, FEATS), BF16),
            vmem((TOKENS, FEATS), BF16),
            vmem((TOKENS, STATE), BF16),
            vmem((TOKENS, STATE), BF16),
            vmem((HEADS, TOKENS), F32),
                vmem((SPANS, SPAN, HEADS), F32),
            vmem((SPANS, HEADS, SPAN), F32),
            vmem((SPANS, SPAN, FEATS), F32),
            vmem((SPANS, SPAN, FEATS), F32),
            vmem((SPANS + 1, STATE, FEATS), F32),
            vmem((SPANS + 1, 8, FEATS), F32),
            vmem((SPAN, FEATS), BF16),
            vmem((7, 2, SPAN, FEATS), BF16),
            vmem((4, 4, 2, SPAN, 128), BF16),
            vmem((4, 4, 2, SPAN, 128), BF16),
            vmem((MESSAGE, HALF), BF16),
            vmem((MESSAGE, HALF), BF16),
            vmem((4, MESSAGE, 128), BF16),
            vmem((4, MESSAGE, 128), BF16),
            vmem((4, MESSAGE, 128), BF16),
            vmem((4, STATE, 128), BF16),
            vmem((4, STATE, 128), BF16),
            vmem((STATE, HALF), BF16),
            vmem((2, STATE, HALF), BF16),
            dma((6,)),
            dma, dma, dma((2, 4)), dma((2, 4)), dma((2, 4, 4)), dma((2, 4, 4)),
            dma((11,)), dma((11,)),
            dma((4,)), dma((4,)),
            dma((7,)), dma((7,)),
            dma((4, 4, 2)), dma((4, 4, 2)),
            dma((4, 4)), dma((4, 4)), dma((4, 4)),
        ],
        compiler_params=pltpu.CompilerParams(
            collective_id=0, has_side_effects=True, vmem_limit_bytes=60 << 20
        ),
        cost_estimate=pl.CostEstimate(flops=11 * 10**9, bytes_accessed=12 << 20, transcendentals=4 << 20),
        name="spanned_mixer",
    )(head_inputs, gate_input, state_write, state_read, log_decay.T, norm_gain.reshape(1, -1), out_weight)
    return (residual.astype(F32) + (kept.astype(F32) + got.astype(F32))).astype(BF16)


def solution(mesh):
    placed = (
        P("ctx", ("segment", "mp")),
        P("ctx", ("segment", "mp")),
        P("ctx", ("segment", "mp")),
        P("ctx", ("segment", "mp")),
        P("ctx", ("segment", "mp")),
        P(("segment", "mp")),
        P(("segment", "mp"), "ctx"),
        P(("ctx", "segment", "mp"), None),
    )
    return jax.shard_map(
        per_device,
        mesh=mesh,
        in_specs=placed,
        out_specs=P(("ctx", "segment", "mp"), None),
        check_vma=False,
    )
```

time: 122 us -> 98.6 us (0.81)
  Pallas kernels: 116 us -> 93.7 us
  local copies, waits for them, and re-layouts: 4.97 us -> 0.01 us
  other arithmetic: 0 us -> 4.69 us
    pallas_call x1, Pallas kernels: 116 us -> 93.7 us  [per_device(): pl.pallas_call(kernel, out_shape=[jax.ShapeDtypeStruct(residual.shape, BF...]
    unnamed x2, local copies, waits for them, and re-layouts: 4.97 us -> 0.01 us
    convert_element_type x0 -> x1, other arithmetic: none -> 4.69 us  [per_device(): (residual.astype(F32) + (kept.astype(F32) + got.astype(F32))).astype(BF16)]
where the time goes in v2:
time: 98.6 us; the launch traced here: 98.4 us
  Pallas kernels  93.7 us (95%)
  other arithmetic  4.69 us (5%)
    pallas_call x1, Pallas kernels, per_device(): pl.pallas_call(kernel, out_shape=[jax.ShapeDtypeStruct(residual.shape, BF...  93.7 us
    convert_element_type x1, other arithmetic, per_device(): (residual.astype(F32) + (kept.astype(F32) + got.astype(F32))).astype(BF16)  4.69 us

profile of v2, /device:TPU:1, one launch (start us, length us, event | category | flops | bytes accessed | tf_op | source)
XLA Modules:
  0.0 98.4 jit_solution(4842726076843709276)
XLA Ops:
  0.0 0.0 copy-start
  0.0 93.7 %spanned_mixer.1 = (bf16[256,4096]{1,0:T(8,128)(2,1)}, bf16[256,4096]{1,0:T(8,128)(2,1)}) custom-call(bf16[1024,1024]{1,0:T(8,128)(2,1)} %x_ref.1, bf16[1024,1024]{1,0:T(8,128)(2,1)} %gate_ref.1, bf16[1024,128]{1,0:T(8,128)(2,1)} %b_ref.1, bf16[1024,128]{1,0:T(8,128)(2,1)} %c_ref.1, f32[16,1024]{1,0:T(8,128)} %bitcast.2, f32[1,1024]{1,0:T(1,128)} %bitcast.3, ...), custom_call_target="tpu_custom_call" | custom-call | flops 11000000512 | bytes 12582912 | tf_op jit(solution)/shard_map/spanned_mixer/pallas_call | solution.py:435
  93.7 0.0 copy-done
  93.8 4.7 %add_convert_fusion = bf16[256,4096]{1,0:T(8,128)(2,1)} fusion(bf16[256,4096]{1,0:T(8,128)(2,1)} %get-tuple-element.8, bf16[256,4096]{1,0:T(8,128)(2,1)} %get-tuple-element.7, bf16[256,4096]{1,0:T(8,128)(2,1)S(1)} %copy-done), kind=kLoop, calls=%fused_computation | loop fusion | flops 6291456 | bytes 8388608 | tf_op jit(solution)/shard_map/convert_element_type | solution.py:480
Async XLA Ops:
  0.0 93.7 %copy-start = (bf16[256,4096]{1,0:T(8,128)(2,1)S(1)}, bf16[256,4096]{1,0:T(8,128)(2,1)}, u32[]{:S(2)}) copy-start(bf16[256,4096]{1,0:T(8,128)(2,1)} %param.15) | copy-start | bytes 6291460

commit v3 on v2

--- a/solution.py
+++ b/solution.py
@@ -50,8 +50,8 @@
 
 
 class RingGather:
-    def __init__(self, W, pos, index, axis, send, recv, sent):
-        self.W, self.pos, self.index, self.axis = W, pos, index, axis
+    def __init__(self, W, pos, index, axis, first, send, recv, sent):
+        self.W, self.pos, self.index, self.axis, self.first = W, pos, index, axis, first
         self.send, self.recv, self.sent = send, recv, sent
         me = pos[axis]
         self.me, self.left, self.right, self.far = me, around(me, 3), around(me, 1), around(me, 2)
@@ -59,7 +59,7 @@
     def copy(self, who, half, distance, k):
         index = list(self.index)
         index[self.axis] = who
-        first, count = (0, 1024) if half is None else (512 * half, 512)
+        first, count = (self.first, 512) if half is None else (self.first + 256 * half, 256)
         ref = self.W.at[tuple(index) + (pl.ds(first, count), ALL)]
         return pltpu.make_async_remote_copy(
             src_ref=ref, dst_ref=ref, send_sem=self.send(k), recv_sem=self.recv(k),
@@ -87,8 +87,8 @@
 
 
 def kernel(
-    x_ref, gate_ref, b_ref, c_ref, ld_ref, gain_ref, w_ref, kept_ref, got_ref,
-    W, X, G, B, C, LD, cum_s, cum_t, ecx, within, ent, thr, NB, ACT, away, keep,
+    x_ref, gate_ref, b_ref, c_ref, ld_ref, gain_ref, w_ref, res_ref, kept_ref, got_ref,
+    W, X, G, B, C, LD, RES, cum_s, cum_t, ecx, within, ent, thr, NB, ACT, away, keep, kin,
     sib_out, sib_in, row_out, row_in, col, back_out, back_in, inc_out, inc,
     load_sem, s0, r0, s1, r1, s2, r2, sx, rx, sa, ra, sf, rf, sr, rr, sk, rk, out_sem,
 ):
@@ -99,7 +99,7 @@
 
     loads = []
     for i, (src, dst) in enumerate((
-        (ld_ref, LD), (w_ref, W.at[x, y, 0]), (x_ref, X), (b_ref, B), (c_ref, C), (gate_ref, G),
+        (ld_ref, LD), (w_ref, W.at[x, y, 0]), (x_ref, X), (b_ref, B), (c_ref, C), (gate_ref, G), (res_ref, RES),
     )):
         loads.append(pltpu.make_async_copy(src, dst, load_sem.at[i]))
         loads[-1].start()
@@ -129,13 +129,15 @@
         return lambda k: array.at[(*at, k)]
 
     ph1, ph2 = [], []
-    for slot, (a1, a2) in enumerate(((1, 0), (0, 1))):
-        ph1.append(RingGather(W, pos, [x, y, slot], a1, sems(s1, slot), sems(r1, slot), sent))
+    for part in range(4):
+        slot, first = part // 2, part % 2 * 512
+        a1, a2 = (1, 0) if part % 2 == 0 else (0, 1)
+        ph1.append(RingGather(W, pos, [x, y, slot], a1, first, sems(s1, part), sems(r1, part), sent))
         subs = []
         for j, d in enumerate((0, 3, 1, 2)):
             index = [x, y, slot]
             index[a1] = around(pos[a1], d)
-            subs.append(RingGather(W, pos, index, a2, sems(s2, slot, j), sems(r2, slot, j), sent))
+            subs.append(RingGather(W, pos, index, a2, first, sems(s2, part, j), sems(r2, part, j), sent))
         ph2.append(subs)
 
     tri_r = lax.broadcasted_iota(jnp.int32, (SPAN, SPAN), 0)
@@ -163,7 +165,9 @@
     zp = around(z, (1 - odd_y) * (3 - 2 * even) + odd_y * (1 + 2 * even))
     push(W.at[x, y, 0], W.at[x, y, 1], s0, r0, device(x, y, zp, c))
     ph1[0].start()
+    ph1[1].start()
     ph2[0][0].start()
+    ph2[1][0].start()
 
     ent[0] = jnp.zeros((STATE, FEATS), F32)
     thr[0] = jnp.ones((8, FEATS), F32)
@@ -199,7 +203,7 @@
     sib_out[:STATE], sib_out[STATE:] = message(ent[SPANS, :, other], thr[SPANS, 0:1, other])
     push(sib_out, sib_in, sx.at[0], rx.at[0], sibling)
 
-    for i in (4,):
+    for i in (4, 5):
         loads[i].wait()
 
     lane_low = lax.broadcasted_iota(jnp.int32, (128, 128), 1) < HEAD_DIM
@@ -210,6 +214,9 @@
         scores = jnp.where(lower, scores, 0.0)
         top, bottom = scores[:128, :128], scores[128:, :]
         cum, cum_row = cum_s[s], cum_t[s]
+        g = G[rows, :].astype(F32)
+        silu = g / (1.0 + jnp.exp(-g))
+        ecx[s] = ecx[s] * silu
         for pair in range(HEADS // 2):
             lanes = slice(pair * 128, (pair + 1) * 128)
             xs = X[rows, lanes]
@@ -220,12 +227,8 @@
                 tops.append(dot(mix, xs[:128]))
                 mix = (jnp.exp(jnp.minimum(col[128:] - row, 0.0)) * bottom).astype(BF16)
                 bottoms.append(dot(mix, xs))
-            within[s, :128, lanes] = jnp.where(lane_low, tops[0], tops[1])
-            within[s, 128:, lanes] = jnp.where(lane_low, bottoms[0], bottoms[1])
-
-    arrived(W.at[x, y, 1], s0, r0)
-    ph1[1].start()
-    ph2[1][0].start()
+            within[s, :128, lanes] = jnp.where(lane_low, tops[0], tops[1]) * silu[:128, lanes]
+            within[s, 128:, lanes] = jnp.where(lane_low, bottoms[0], bottoms[1]) * silu[128:, lanes]
 
     arrived(sib_in, sx.at[0], rx.at[0])
     first_core = c == 0
@@ -243,10 +246,9 @@
         to = around(y, i)
         push(row_out.at[to], row_in.at[y], sx.at[i], rx.at[i], shifted(pos, 1, i))
     row_in[y] = row_out[y]
-
+    ph1[1].forward()
     ph1[0].forward()
     ph2[0][1].start()
-    ph2[0][2].start()
 
     within_span(0)
 
@@ -263,11 +265,11 @@
     for i in (2, 1, 3):
         push(col.at[x], col.at[x], sx.at[3 + i], rx.at[3 + i], shifted(pos, 0, i))
 
-    ph1[1].forward()
-    ph2[1][1].start()
-    ph2[1][2].start()
+    arrived(W.at[x, y, 1], s0, r0)
+    ph1[2].start()
+    ph1[3].start()
     ph1[0].finish()
-    ph2[0][3].start()
+    ph1[1].finish()
 
     within_span(1)
 
@@ -284,8 +286,12 @@
         push(back_out.at[to], back_in.at[y], sx.at[6 + i], rx.at[6 + i], shifted(pos, 1, i))
     back_in[y] = back_out[y]
 
-    ph1[1].finish()
-    ph2[1][3].start()
+    ph1[3].forward()
+    ph1[2].forward()
+    for j in (1, 2, 3):
+        ph2[1][j].start()
+        if j > 1:
+            ph2[0][j].start()
 
     within_span(2)
 
@@ -297,28 +303,29 @@
     inc_out[...] = jnp.where(first_core, enter1, enter0).astype(BF16)
     push(inc_out, inc.at[c], sx.at[10], rx.at[10], sibling)
 
-    for t in ph2:
-        t[0].forward()
+    ph1[2].finish()
+    ph1[3].finish()
+    ph2[0][0].forward()
+    ph2[1][0].forward()
 
     within_span(3)
 
-    for i in (5,):
-        loads[i].wait()
     arrived(inc.at[1 - c], sx.at[10], rx.at[10])
 
     def normed(q):
         rows = pl.ds(pl.multiple_of(q * SPAN, SPAN), SPAN)
         incoming = jnp.concatenate([inc[0], inc[1]], axis=1).astype(F32)
         state = (ent[q] + thr[q, 0:1, :] * incoming).astype(BF16)
-        mixed = within[q] + dot(C[rows, :], state) * ecx[q]
-        g = G[rows, :].astype(F32)
-        gated = mixed * (g / (1.0 + jnp.exp(-g)))
+        gated = within[q] + dot(C[rows, :], state) * ecx[q]
         factor = lax.rsqrt(jnp.mean(gated * gated, axis=1, keepdims=True) + 1e-05)
         return (gated * factor * gain_ref[...]).astype(BF16)
 
     NB[...] = normed(zo)
     push(NB, ACT.at[3, c], sa.at[0], ra.at[0], device(x, y, za, c))
     push(NB, ACT.at[4, c], sa.at[1], ra.at[1], device(x, y, zb, c))
+    for j in range(4):
+        ph2[2][j].start()
+        ph2[3][j].start()
     ACT[1, c] = normed(za)
     push(ACT.at[1, c], ACT.at[5, c], sa.at[2], ra.at[2], device(x, y, za, c))
     ACT[2, c] = normed(zb)
@@ -333,19 +340,22 @@
     share(0)
 
     for j in (1, 2, 3):
-        for t in ph2:
-            t[j].forward()
+        ph2[0][j].forward()
+        ph2[1][j].forward()
 
     for i in (0, 1):
         arrived(ACT.at[3 + i, c], sa.at[i], ra.at[i])
         share(3 + i)
+    for j in range(4):
+        ph2[2][j].forward()
+        ph2[3][j].forward()
     for slot in (1, 2, 3, 4):
         arrived(ACT.at[slot, 1 - c], sf.at[slot], rf.at[slot])
 
     def product(own, other, b0, b1):
         lhs = jnp.concatenate([ACT[own].reshape(2 * SPAN, FEATS), ACT[other].reshape(2 * SPAN, FEATS)], axis=1)
         rhs = jnp.concatenate([W[b[0], b[1]].reshape(2 * FEATS, 128) for b in (b0, b1)], axis=1)
-        return dot(lhs, rhs).astype(BF16)
+        return dot(lhs, rhs)
 
     def columns(bx, by, core):
         return pl.ds(pl.multiple_of((bx * 8 + by * 2 + core) * 128, 128), 128)
@@ -359,12 +369,9 @@
             device_id=device(x, y, target, section), device_id_type=MESH,
         )
 
-    def keep_local(bx, by):
-        return pltpu.make_async_copy(keep.at[bx, by, c], kept_ref.at[:, columns(bx, by, c)], out_sem.at[bx, by])
-
     def keep_remote(bx, by):
         return pltpu.make_async_remote_copy(
-            src_ref=keep.at[bx, by, 1 - c], dst_ref=kept_ref.at[:, columns(bx, by, c)],
+            src_ref=keep.at[bx, by], dst_ref=kin.at[bx, by],
             send_sem=sk.at[bx, by], recv_sem=rk.at[bx, by], device_id=sibling, device_id_type=MESH,
         )
 
@@ -387,44 +394,55 @@
         result = product(2 - odd, 3 + odd, b0, b1)
         for k, (bx, by) in enumerate((b0, b1)):
             for section in (0, 1):
-                away[bx, by, section] = result[section * SPAN:(section + 1) * SPAN, k * 128:(k + 1) * 128]
+                away[bx, by, section] = result[section * SPAN:(section + 1) * SPAN, k * 128:(k + 1) * 128].astype(BF16)
                 away_copy(bx, by, section).start()
 
     def keep_here(b0, b1):
         odd = lax.rem(b0[1], 2)
         result = product(0, 5 + odd, b0, b1)
         for k, (bx, by) in enumerate((b0, b1)):
-            for section in (0, 1):
-                keep[bx, by, section] = result[section * SPAN:(section + 1) * SPAN, k * 128:(k + 1) * 128]
+            parts = [result[section * SPAN:(section + 1) * SPAN, k * 128:(k + 1) * 128] for section in (0, 1)]
+            keep[bx, by] = jnp.where(first_core, parts[1], parts[0]).astype(BF16)
             keep_remote(bx, by).start()
-            keep_local(bx, by).start()
+            lanes = columns(bx, by, c)
+            RES[:, lanes] = (RES[:, lanes].astype(F32) + jnp.where(first_core, parts[0], parts[1])).astype(BF16)
 
     over_pairs(near, send_away)
-    for t in ph2:
-        for j in range(4):
-            t[j].finish()
-    over_pairs(rest, send_away)
     for i in (2, 3):
         arrived(ACT.at[3 + i, c], sa.at[i], ra.at[i])
         share(3 + i)
     for slot in (0, 5, 6):
         arrived(ACT.at[slot, 1 - c], sf.at[slot], rf.at[slot])
+    loads[6].wait()
     over_pairs(near, keep_here)
+    for t in ph2:
+        for j in range(4):
+            t[j].finish()
+    over_pairs(rest, send_away)
     over_pairs(rest, keep_here)
 
     @pl.loop(0, 16)
     def _(i):
         bx, by = lax.div(i, 4), lax.rem(i, 4)
-        keep_local(bx, by).wait()
         keep_remote(bx, by).wait_send()
-        arrived(kept_ref.at[:, columns(bx, by, 1 - c)], sk.at[bx, by], rk.at[bx, by])
+        arrived(kin.at[bx, by], sk.at[bx, by], rk.at[bx, by])
+        lanes = columns(bx, by, 1 - c)
+        RES[:, lanes] = (RES[:, lanes].astype(F32) + kin[bx, by].astype(F32)).astype(BF16)
+
+    kept_copy = pltpu.make_async_copy(RES, kept_ref, out_sem)
+    kept_copy.start()
+
+    for cp in sent:
+        cp.wait_send()
+    kept_copy.wait()
+
+    @pl.loop(0, 16)
+    def _(i):
+        bx, by = lax.div(i, 4), lax.rem(i, 4)
         for section in (0, 1):
             away_copy(bx, by, section).wait_send()
         for core in (0, 1):
             arrived(got_ref.at[:, columns(bx, by, core)], sr.at[bx, by, core], rr.at[bx, by, core])
-
-    for cp in sent:
-        cp.wait_send()
 
 
 def per_device(
@@ -435,7 +453,7 @@
     kept, got = pl.pallas_call(
         kernel,
         out_shape=[jax.ShapeDtypeStruct(residual.shape, BF16)] * 2,
-        in_specs=[any_space] * 5 + [pl.BlockSpec(memory_space=pltpu.VMEM)] + [any_space],
+        in_specs=[any_space] * 5 + [pl.BlockSpec(memory_space=pltpu.VMEM)] + [any_space] * 2,
         out_specs=[any_space] * 2,
         scratch_shapes=[
             vmem((4, 4, 2, 1024, 128), BF16),
@@ -444,6 +462,7 @@
             vmem((TOKENS, STATE), BF16),
             vmem((TOKENS, STATE), BF16),
             vmem((HEADS, TOKENS), F32),
+            vmem((SPAN, 4096), BF16),
                 vmem((SPANS, SPAN, HEADS), F32),
             vmem((SPANS, HEADS, SPAN), F32),
             vmem((SPANS, SPAN, FEATS), F32),
@@ -453,7 +472,8 @@
             vmem((SPAN, FEATS), BF16),
             vmem((7, 2, SPAN, FEATS), BF16),
             vmem((4, 4, 2, SPAN, 128), BF16),
-            vmem((4, 4, 2, SPAN, 128), BF16),
+            vmem((4, 4, SPAN, 128), BF16),
+            vmem((4, 4, SPAN, 128), BF16),
             vmem((MESSAGE, HALF), BF16),
             vmem((MESSAGE, HALF), BF16),
             vmem((4, MESSAGE, 128), BF16),
@@ -463,21 +483,21 @@
             vmem((4, STATE, 128), BF16),
             vmem((STATE, HALF), BF16),
             vmem((2, STATE, HALF), BF16),
-            dma((6,)),
-            dma, dma, dma((2, 4)), dma((2, 4)), dma((2, 4, 4)), dma((2, 4, 4)),
+            dma((7,)),
+            dma, dma, dma((4, 4)), dma((4, 4)), dma((4, 4, 4)), dma((4, 4, 4)),
             dma((11,)), dma((11,)),
             dma((4,)), dma((4,)),
             dma((7,)), dma((7,)),
             dma((4, 4, 2)), dma((4, 4, 2)),
-            dma((4, 4)), dma((4, 4)), dma((4, 4)),
+            dma((4, 4)), dma((4, 4)), dma,
         ],
         compiler_params=pltpu.CompilerParams(
             collective_id=0, has_side_effects=True, vmem_limit_bytes=60 << 20
         ),
         cost_estimate=pl.CostEstimate(flops=11 * 10**9, bytes_accessed=12 << 20, transcendentals=4 << 20),
         name="spanned_mixer",
-    )(head_inputs, gate_input, state_write, state_read, log_decay.T, norm_gain.reshape(1, -1), out_weight)
-    return (residual.astype(F32) + (kept.astype(F32) + got.astype(F32))).astype(BF16)
+    )(head_inputs, gate_input, state_write, state_read, log_decay.T, norm_gain.reshape(1, -1), out_weight, residual)
+    return (kept.astype(F32) + got.astype(F32)).astype(BF16)
 
 
 def solution(mesh):

time: 98.6 us -> 86.9 us (0.88)
  Pallas kernels: 93.7 us -> 82.4 us
    pallas_call x1, Pallas kernels: 93.7 us -> 82.4 us  [per_device(): pl.pallas_call(kernel, out_shape=[jax.ShapeDtypeStruct(residual.shape, BF...]
where the time goes in v3:
time: 86.9 us; the launch traced here: 86.8 us
  Pallas kernels  82.4 us (95%)
  other arithmetic  4.33 us (5%)
    pallas_call x1, Pallas kernels, per_device(): pl.pallas_call(kernel, out_shape=[jax.ShapeDtypeStruct(residual.shape, BF...  82.4 us
    convert_element_type x1, other arithmetic, per_device(): return (kept.astype(F32) + got.astype(F32)).astype(BF16)  4.33 us

profile of v3, /device:TPU:1, one launch (start us, length us, event | category | flops | bytes accessed | tf_op | source)
XLA Modules:
  0.0 86.8 jit_solution(13287788441465439666)
XLA Ops:
  0.0 82.4 %spanned_mixer.1 = (bf16[256,4096]{1,0:T(8,128)(2,1)}, bf16[256,4096]{1,0:T(8,128)(2,1)}) custom-call(bf16[1024,1024]{1,0:T(8,128)(2,1)} %x_ref.1, bf16[1024,1024]{1,0:T(8,128)(2,1)} %gate_ref.1, bf16[1024,128]{1,0:T(8,128)(2,1)} %b_ref.1, bf16[1024,128]{1,0:T(8,128)(2,1)} %c_ref.1, f32[16,1024]{1,0:T(8,128)} %bitcast.2, f32[1,1024]{1,0:T(1,128)} %bitcast.3, ...), custom_call_target="tpu_custom_call" | custom-call | flops 11000000512 | bytes 12582912 | tf_op jit(solution)/shard_map/spanned_mixer/pallas_call | solution.py:453
  82.5 4.3 %add_convert_fusion = bf16[256,4096]{1,0:T(8,128)(2,1)} fusion(bf16[256,4096]{1,0:T(8,128)(2,1)} %get-tuple-element.8, bf16[256,4096]{1,0:T(8,128)(2,1)} %get-tuple-element.7), kind=kLoop, calls=%fused_computation | loop fusion | flops 4194304 | bytes 6291456 | tf_op jit(solution)/shard_map/convert_element_type | solution.py:500

commit v4 on v3

--- a/solution.py
+++ b/solution.py
@@ -159,16 +159,6 @@
         cum = dot(hi, tri) + dot(mid, tri) + dot(lo, tri)
         cum_t[s] = cum
         cum_s[s] = cum.T
-    loads[1].wait()
-    pl.semaphore_wait(barrier, len(partners))
-    odd_y = lax.rem(y, 2)
-    zp = around(z, (1 - odd_y) * (3 - 2 * even) + odd_y * (1 + 2 * even))
-    push(W.at[x, y, 0], W.at[x, y, 1], s0, r0, device(x, y, zp, c))
-    ph1[0].start()
-    ph1[1].start()
-    ph2[0][0].start()
-    ph2[1][0].start()
-
     ent[0] = jnp.zeros((STATE, FEATS), F32)
     thr[0] = jnp.ones((8, FEATS), F32)
     for i in (2, 3):
@@ -187,6 +177,15 @@
 
     for s in range(SPANS):
         fresh(s)
+
+    loads[1].wait()
+    pl.semaphore_wait(barrier, len(partners))
+    odd_y = lax.rem(y, 2)
+    zp = around(z, (1 - odd_y) * (3 - 2 * even) + odd_y * (1 + 2 * even))
+    push(W.at[x, y, 0], W.at[x, y, 1], s0, r0, device(x, y, zp, c))
+    ph1[0].start()
+    ph1[1].start()
+    ph2[0][0].start()
 
     mine = pl.ds(pl.multiple_of(c * HALF, HALF), HALF)
     other = pl.ds(pl.multiple_of((1 - c) * HALF, HALF), HALF)
@@ -248,7 +247,6 @@
     row_in[y] = row_out[y]
     ph1[1].forward()
     ph1[0].forward()
-    ph2[0][1].start()
 
     within_span(0)
 
@@ -268,7 +266,9 @@
     arrived(W.at[x, y, 1], s0, r0)
     ph1[2].start()
     ph1[3].start()
+    ph2[1][0].start()
     ph1[0].finish()
+    ph2[0][1].start()
     ph1[1].finish()
 
     within_span(1)
@@ -312,17 +312,20 @@
 
     arrived(inc.at[1 - c], sx.at[10], rx.at[10])
 
-    def normed(q):
-        rows = pl.ds(pl.multiple_of(q * SPAN, SPAN), SPAN)
+    def normed(q, first=0, count=SPAN):
+        rows = pl.ds(pl.multiple_of(q * SPAN + first, 128), count)
         incoming = jnp.concatenate([inc[0], inc[1]], axis=1).astype(F32)
         state = (ent[q] + thr[q, 0:1, :] * incoming).astype(BF16)
-        gated = within[q] + dot(C[rows, :], state) * ecx[q]
+        here = slice(first, first + count)
+        gated = within[q, here] + dot(C[rows, :], state) * ecx[q, here]
         factor = lax.rsqrt(jnp.mean(gated * gated, axis=1, keepdims=True) + 1e-05)
         return (gated * factor * gain_ref[...]).astype(BF16)
 
-    NB[...] = normed(zo)
-    push(NB, ACT.at[3, c], sa.at[0], ra.at[0], device(x, y, za, c))
-    push(NB, ACT.at[4, c], sa.at[1], ra.at[1], device(x, y, zb, c))
+    for h in (0, 1):
+        half = slice(h * 128, (h + 1) * 128)
+        NB[half] = normed(zo, h * 128, 128)
+        push(NB.at[half], ACT.at[3, c, half], sa.at[4 * h], ra.at[4 * h], device(x, y, za, c))
+        push(NB.at[half], ACT.at[4, c, half], sa.at[4 * h + 1], ra.at[4 * h + 1], device(x, y, zb, c))
     for j in range(4):
         ph2[2][j].start()
         ph2[3][j].start()
@@ -344,7 +347,8 @@
         ph2[1][j].forward()
 
     for i in (0, 1):
-        arrived(ACT.at[3 + i, c], sa.at[i], ra.at[i])
+        for h in (0, 1):
+            arrived(ACT.at[3 + i, c, h * 128:(h + 1) * 128], sa.at[4 * h + i], ra.at[4 * h + i])
         share(3 + i)
     for j in range(4):
         ph2[2][j].forward()
@@ -411,14 +415,14 @@
     for i in (2, 3):
         arrived(ACT.at[3 + i, c], sa.at[i], ra.at[i])
         share(3 + i)
+    for t in ph2:
+        for j in range(4):
+            t[j].finish()
+    over_pairs(rest, send_away)
     for slot in (0, 5, 6):
         arrived(ACT.at[slot, 1 - c], sf.at[slot], rf.at[slot])
     loads[6].wait()
     over_pairs(near, keep_here)
-    for t in ph2:
-        for j in range(4):
-            t[j].finish()
-    over_pairs(rest, send_away)
     over_pairs(rest, keep_here)
 
     @pl.loop(0, 16)
@@ -486,7 +490,7 @@
             dma((7,)),
             dma, dma, dma((4, 4)), dma((4, 4)), dma((4, 4, 4)), dma((4, 4, 4)),
             dma((11,)), dma((11,)),
-            dma((4,)), dma((4,)),
+            dma((6,)), dma((6,)),
             dma((7,)), dma((7,)),
             dma((4, 4, 2)), dma((4, 4, 2)),
             dma((4, 4)), dma((4, 4)), dma,

time: 86.9 us -> 84.2 us (0.969)
  Pallas kernels: 82.4 us -> 79.7 us
    pallas_call x1, Pallas kernels: 82.4 us -> 79.7 us  [per_device(): pl.pallas_call(kernel, out_shape=[jax.ShapeDtypeStruct(residual.shape, BF...]
where the time goes in v4:
time: 84.2 us; the launch traced here: 84.1 us
  Pallas kernels  79.7 us (95%)
  other arithmetic  4.33 us (5%)
    pallas_call x1, Pallas kernels, per_device(): pl.pallas_call(kernel, out_shape=[jax.ShapeDtypeStruct(residual.shape, BF...  79.7 us
    convert_element_type x1, other arithmetic, per_device(): return (kept.astype(F32) + got.astype(F32)).astype(BF16)  4.33 us

profile of v4, /device:TPU:1, one launch (start us, length us, event | category | flops | bytes accessed | tf_op | source)
XLA Modules:
  0.0 84.1 jit_solution(17267217730653841890)
XLA Ops:
  0.0 79.7 %spanned_mixer.1 = (bf16[256,4096]{1,0:T(8,128)(2,1)}, bf16[256,4096]{1,0:T(8,128)(2,1)}) custom-call(bf16[1024,1024]{1,0:T(8,128)(2,1)} %x_ref.1, bf16[1024,1024]{1,0:T(8,128)(2,1)} %gate_ref.1, bf16[1024,128]{1,0:T(8,128)(2,1)} %b_ref.1, bf16[1024,128]{1,0:T(8,128)(2,1)} %c_ref.1, f32[16,1024]{1,0:T(8,128)} %bitcast.2, f32[1,1024]{1,0:T(1,128)} %bitcast.3, ...), custom_call_target="tpu_custom_call" | custom-call | flops 11000000512 | bytes 12582912 | tf_op jit(solution)/shard_map/spanned_mixer/pallas_call | solution.py:457
  79.7 4.3 %add_convert_fusion = bf16[256,4096]{1,0:T(8,128)(2,1)} fusion(bf16[256,4096]{1,0:T(8,128)(2,1)} %get-tuple-element.8, bf16[256,4096]{1,0:T(8,128)(2,1)} %get-tuple-element.7), kind=kLoop, calls=%fused_computation | loop fusion | flops 4194304 | bytes 6291456 | tf_op jit(solution)/shard_map/convert_element_type | solution.py:504

commit v5 on v4

--- a/solution.py
+++ b/solution.py
@@ -181,8 +181,21 @@
     loads[1].wait()
     pl.semaphore_wait(barrier, len(partners))
     odd_y = lax.rem(y, 2)
-    zp = around(z, (1 - odd_y) * (3 - 2 * even) + odd_y * (1 + 2 * even))
-    push(W.at[x, y, 0], W.at[x, y, 1], s0, r0, device(x, y, zp, c))
+
+    def sharer(odd):
+        return device(x, y, around(z, (1 - odd) * (3 - 2 * even) + odd * (1 + 2 * even)), c)
+
+    push(W.at[x, y, 0], W.at[x, y, 1], s0, r0, sharer(odd_y))
+
+    def half_block(k, slot):
+        d = (3, 1, 2)[k % 3]
+        bx, by = (x, around(y, d)) if k < 3 else (around(x, d), y)
+        return W.at[bx, by, slot, pl.ds(k // 3 * 512, 512)], lax.rem(by, 2)
+
+    def hand(k):
+        src, odd = half_block(k, 0)
+        push(src, half_block(k, 1)[0], s1.at[2 + k // 3, k % 3], r1.at[2 + k // 3, k % 3], sharer(odd))
+
     ph1[0].start()
     ph1[1].start()
     ph2[0][0].start()
@@ -247,6 +260,8 @@
     row_in[y] = row_out[y]
     ph1[1].forward()
     ph1[0].forward()
+    for k in (3, 4, 0, 1):
+        hand(k)
 
     within_span(0)
 
@@ -263,13 +278,12 @@
     for i in (2, 1, 3):
         push(col.at[x], col.at[x], sx.at[3 + i], rx.at[3 + i], shifted(pos, 0, i))
 
-    arrived(W.at[x, y, 1], s0, r0)
-    ph1[2].start()
-    ph1[3].start()
     ph2[1][0].start()
     ph1[0].finish()
     ph2[0][1].start()
     ph1[1].finish()
+    for k in (5, 2):
+        hand(k)
 
     within_span(1)
 
@@ -286,8 +300,6 @@
         push(back_out.at[to], back_in.at[y], sx.at[6 + i], rx.at[6 + i], shifted(pos, 1, i))
     back_in[y] = back_out[y]
 
-    ph1[3].forward()
-    ph1[2].forward()
     for j in (1, 2, 3):
         ph2[1][j].start()
         if j > 1:
@@ -303,8 +315,6 @@
     inc_out[...] = jnp.where(first_core, enter1, enter0).astype(BF16)
     push(inc_out, inc.at[c], sx.at[10], rx.at[10], sibling)
 
-    ph1[2].finish()
-    ph1[3].finish()
     ph2[0][0].forward()
     ph2[1][0].forward()
 
@@ -326,6 +336,9 @@
         NB[half] = normed(zo, h * 128, 128)
         push(NB.at[half], ACT.at[3, c, half], sa.at[4 * h], ra.at[4 * h], device(x, y, za, c))
         push(NB.at[half], ACT.at[4, c, half], sa.at[4 * h + 1], ra.at[4 * h + 1], device(x, y, zb, c))
+    arrived(W.at[x, y, 1], s0, r0)
+    for k in range(6):
+        arrived(half_block(k, 1)[0], s1.at[2 + k // 3, k % 3], r1.at[2 + k // 3, k % 3])
     for j in range(4):
         ph2[2][j].start()
         ph2[3][j].start()

time: 84.2 us -> 83.1 us (0.987)
  Pallas kernels: 79.7 us -> 78.6 us
    pallas_call x1, Pallas kernels: 79.7 us -> 78.6 us  [per_device(): pl.pallas_call(kernel, out_shape=[jax.ShapeDtypeStruct(residual.shape, BF...]
where the time goes in v5:
time: 83.1 us; the launch traced here: 82.9 us
  Pallas kernels  78.6 us (95%)
  other arithmetic  4.33 us (5%)
    pallas_call x1, Pallas kernels, per_device(): pl.pallas_call(kernel, out_shape=[jax.ShapeDtypeStruct(residual.shape, BF...  78.6 us
    convert_element_type x1, other arithmetic, per_device(): return (kept.astype(F32) + got.astype(F32)).astype(BF16)  4.33 us

profile of v5, /device:TPU:1, one launch (start us, length us, event | category | flops | bytes accessed | tf_op | source)
XLA Modules:
  0.0 82.9 jit_solution(12862705052210467324)
XLA Ops:
  0.0 78.6 %spanned_mixer.1 = (bf16[256,4096]{1,0:T(8,128)(2,1)}, bf16[256,4096]{1,0:T(8,128)(2,1)}) custom-call(bf16[1024,1024]{1,0:T(8,128)(2,1)} %x_ref.1, bf16[1024,1024]{1,0:T(8,128)(2,1)} %gate_ref.1, bf16[1024,128]{1,0:T(8,128)(2,1)} %b_ref.1, bf16[1024,128]{1,0:T(8,128)(2,1)} %c_ref.1, f32[16,1024]{1,0:T(8,128)} %bitcast.2, f32[1,1024]{1,0:T(1,128)} %bitcast.3, ...), custom_call_target="tpu_custom_call" | custom-call | flops 11000000512 | bytes 12582912 | tf_op jit(solution)/shard_map/spanned_mixer/pallas_call | solution.py:470
  78.6 4.3 %add_convert_fusion = bf16[256,4096]{1,0:T(8,128)(2,1)} fusion(bf16[256,4096]{1,0:T(8,128)(2,1)} %get-tuple-element.8, bf16[256,4096]{1,0:T(8,128)(2,1)} %get-tuple-element.7), kind=kLoop, calls=%fused_computation | loop fusion | flops 4194304 | bytes 6291456 | tf_op jit(solution)/shard_map/convert_element_type | solution.py:517

commit v6 on v5

--- a/solution.py
+++ b/solution.py
@@ -320,6 +320,13 @@
 
     within_span(3)
 
+    arrived(W.at[x, y, 1], s0, r0)
+    for k in range(6):
+        arrived(half_block(k, 1)[0], s1.at[2 + k // 3, k % 3], r1.at[2 + k // 3, k % 3])
+    for j in range(4):
+        ph2[2][j].start()
+        ph2[3][j].start()
+
     arrived(inc.at[1 - c], sx.at[10], rx.at[10])
 
     def normed(q, first=0, count=SPAN):
@@ -336,12 +343,6 @@
         NB[half] = normed(zo, h * 128, 128)
         push(NB.at[half], ACT.at[3, c, half], sa.at[4 * h], ra.at[4 * h], device(x, y, za, c))
         push(NB.at[half], ACT.at[4, c, half], sa.at[4 * h + 1], ra.at[4 * h + 1], device(x, y, zb, c))
-    arrived(W.at[x, y, 1], s0, r0)
-    for k in range(6):
-        arrived(half_block(k, 1)[0], s1.at[2 + k // 3, k % 3], r1.at[2 + k // 3, k % 3])
-    for j in range(4):
-        ph2[2][j].start()
-        ph2[3][j].start()
     ACT[1, c] = normed(za)
     push(ACT.at[1, c], ACT.at[5, c], sa.at[2], ra.at[2], device(x, y, za, c))
     ACT[2, c] = normed(zb)

time: 83.1 us -> 83.1 us (level)
  no operation moved by 1% of the time
where the time goes in v6:
time: 83.1 us; the launch traced here: 82.9 us
  Pallas kernels  78.6 us (95%)
  other arithmetic  4.33 us (5%)
    pallas_call x1, Pallas kernels, per_device(): pl.pallas_call(kernel, out_shape=[jax.ShapeDtypeStruct(residual.shape, BF...  78.6 us
    convert_element_type x1, other arithmetic, per_device(): return (kept.astype(F32) + got.astype(F32)).astype(BF16)  4.33 us

profile of v6, /device:TPU:1, one launch (start us, length us, event | category | flops | bytes accessed | tf_op | source)
XLA Modules:
  0.0 82.9 jit_solution(8402492556393526984)
XLA Ops:
  0.0 78.6 %spanned_mixer.1 = (bf16[256,4096]{1,0:T(8,128)(2,1)}, bf16[256,4096]{1,0:T(8,128)(2,1)}) custom-call(bf16[1024,1024]{1,0:T(8,128)(2,1)} %x_ref.1, bf16[1024,1024]{1,0:T(8,128)(2,1)} %gate_ref.1, bf16[1024,128]{1,0:T(8,128)(2,1)} %b_ref.1, bf16[1024,128]{1,0:T(8,128)(2,1)} %c_ref.1, f32[16,1024]{1,0:T(8,128)} %bitcast.2, f32[1,1024]{1,0:T(1,128)} %bitcast.3, ...), custom_call_target="tpu_custom_call" | custom-call | flops 11000000512 | bytes 12582912 | tf_op jit(solution)/shard_map/spanned_mixer/pallas_call | solution.py:471
  78.6 4.3 %add_convert_fusion = bf16[256,4096]{1,0:T(8,128)(2,1)} fusion(bf16[256,4096]{1,0:T(8,128)(2,1)} %get-tuple-element.8, bf16[256,4096]{1,0:T(8,128)(2,1)} %get-tuple-element.7), kind=kLoop, calls=%fused_computation | loop fusion | flops 4194304 | bytes 6291456 | tf_op jit(solution)/shard_map/convert_element_type | solution.py:518
